TPU v7x, 512 devices: a whole 4x8x8 slice. The times are simulated.
512 devices in a mesh: section: 16 (over z, core), dp: 32 (over x, y).
Axes of the slice: x: 4, y: 8, z: 8, core: 2. Of those that a mesh axis runs over, the one named last changes fastest.
Arguments:
- grads: bfloat16 [16, 32, 80, 8192], P('section', 'dp'), may hold values from -6400 to 6400
- owners: int32 [16, 24], P('section'), may hold values from 0 to 31, as said below
- master: float32 [16, 32, 8, 8192], P('section', 'dp'), may hold values from -0.008 to 0.008
- moment: float32 [16, 32, 8, 8192], P('section', 'dp'), may hold values from -4 to 4
- second: float32 [16, 32, 8, 8192], P('section', 'dp'), may hold values from 0.01 to 1
- average: float32 [16, 32, 8, 8192], P('section', 'dp'), may hold values from -0.0001 to 0.0001
Outputs:
- weights: bfloat16 [16, 80, 8192], P('section')
- master_out: float32 [16, 32, 8, 8192], P('section', 'dp')
- moment_out: float32 [16, 32, 8, 8192], P('section', 'dp')
- second_out: float32 [16, 32, 8, 8192], P('section', 'dp')
- average_out: float32 [16, 32, 8, 8192], P('section', 'dp')
Inputs may be any that keep to these rules, and one draw needn't show every extreme that they name: The 24 tensors of one section have 24 different owners.
All inputs are finite; a program needn't handle non-finite values.
Results may differ from a plain program's by a relative error of at most 0.012.
Values may be sent and summed in bfloat16 or wider, within the bound.
No kernel may reach another device: no remote copies, remote signals or barrier semaphores. Data moves between devices by JAX's collectives and lax.ppermute only.
A program may use at most 64 MiB of HBM per device.

v0:
```python
import jax
import jax.numpy as jnp
from jax import lax
from jax.sharding import PartitionSpec as P

STEP = 10


beta_one = 0.9
beta_two = 0.95
epsilon = 1e-08
learn_rate = 0.0003
decay_rate = 0.1
average_keep = 0.999
clip_level = 0.5


def spread(array, axis, root):
    mine = lax.axis_index(axis) == root
    return lax.psum(jnp.where(mine, array, jnp.zeros_like(array)), axis)


def tensor_layout(all_rows, slot_rows, layers):
    layer_rows = all_rows // layers
    kv_rows = (layer_rows - 2 - 2 * slot_rows) // 2
    counts = [slot_rows, kv_rows, kv_rows, slot_rows, 1, 1]
    layout = []
    start = 0
    for layer in range(layers):
        for position, count in enumerate(counts):
            layout.append((start, count, 1.0 if position < 4 else 0.0))
            start = start + count
    return layout


def adamw(grad, master, moment, second, average, decay, factor):
    clipped = factor * grad
    moment_new = beta_one * moment + (1.0 - beta_one) * clipped
    second_new = beta_two * second + (1.0 - beta_two) * clipped * clipped
    direction = (
        moment_new
        / (1.0 - beta_one**STEP)
        / (jnp.sqrt(second_new / (1.0 - beta_two**STEP)) + epsilon)
    )
    master_new = master - learn_rate * (direction + decay_rate * decay * master)
    average_new = average_keep * average + (1.0 - average_keep) * master_new
    return (master_new, moment_new, second_new, average_new)


def local(grads, owners, master, moment, second, average):
    all_rows = grads.shape[2]
    width = grads.shape[3]
    slot_rows = master.shape[2]
    layer_count = owners.shape[1] // 6
    layout = tensor_layout(all_rows, slot_rows, layer_count)
    owner = owners[0]
    own_index = lax.axis_index("dp")
    replicas = lax.axis_size("dp")
    numel = lax.axis_size("section") * all_rows * width
    flat = grads[0, 0].astype(jnp.float32)
    slot_ids = jnp.arange(slot_rows).reshape(slot_rows, 1)
    used = jnp.zeros((slot_rows, 1), jnp.bool_)
    decay = jnp.zeros((slot_rows, 1), jnp.float32)
    for tensor, (start, count, flag) in enumerate(layout):
        marks = jnp.logical_and(slot_ids < count, owner[tensor] == own_index)
        used = jnp.logical_or(used, marks)
        decay = jnp.where(marks, flag, decay)
    total = lax.psum(flat.astype(jnp.bfloat16), "dp").astype(jnp.float32)
    mean = total / replicas
    squares = lax.psum(jnp.sum(mean * mean), "section")
    bucket = jnp.zeros((slot_rows, width), jnp.float32)
    for tensor, (start, count, flag) in enumerate(layout):
        rows = jnp.pad(mean[start : start + count], ((0, slot_rows - count), (0, 0)))
        marks = jnp.logical_and(slot_ids < count, owner[tensor] == own_index)
        bucket = jnp.where(marks, rows, bucket)
    factor = jnp.minimum(1.0, clip_level / jnp.sqrt(squares / numel + 1e-06))
    olds = (master[0, 0], moment[0, 0], second[0, 0], average[0, 0])
    fresh = adamw(bucket, olds[0], olds[1], olds[2], olds[3], decay, factor)
    kept = tuple(
        (jnp.where(used, new_value, old_value) for new_value, old_value in zip(fresh, olds))
    )
    new_weights = kept[0].astype(jnp.bfloat16)
    pieces = []
    for tensor, (start, count, flag) in enumerate(layout):
        pieces.append(spread(new_weights[:count], "dp", owner[tensor]))
    weights = jnp.concatenate(pieces, axis=0)
    return (
        weights[None],
        kept[0][None, None],
        kept[1][None, None],
        kept[2][None, None],
        kept[3][None, None],
    )


def solution(mesh):
    in_specs = (
        P("section", "dp", None, None),
        P("section", None),
        P("section", "dp", None, None),
        P("section", "dp", None, None),
        P("section", "dp", None, None),
        P("section", "dp", None, None),
    )
    out_specs = (
        P("section", None, None),
        P("section", "dp", None, None),
        P("section", "dp", None, None),
        P("section", "dp", None, None),
        P("section", "dp", None, None),
    )
    return jax.shard_map(local, mesh=mesh, in_specs=in_specs, out_specs=out_specs, check_vma=False)
```

profile of v0, /device:TPU:1, one launch (start us, length us, event | category | flops | bytes accessed | tf_op | source)
XLA Modules:
  0.0 573.6 jit_solution(10690828884362636822)
XLA Ops:
  7.2 0.0 all-reduce.22.cloned.1.call-start
  7.2 0.7 all-reduce.22.cloned.1.call-update
  7.9 0.0 all-reduce.24.cloned.1.call-start
  7.9 1.4 fusion.38
  15.9 2.1 fusion.37
  22.3 0.0 copy-start
  22.3 0.0 copy-start.1
  42.3 0.6 broadcast_and_fusion.22
  42.8 0.6 broadcast_and_fusion
  43.4 0.6 broadcast_and_fusion.2
  44.0 0.6 broadcast_and_fusion.4
  44.6 0.6 broadcast_and_fusion.6
  45.2 0.5 broadcast_and_fusion.8
  45.7 0.6 broadcast_and_fusion.10
  46.3 0.6 broadcast_and_fusion.12
  46.9 0.5 broadcast_and_fusion.14
  47.4 0.6 broadcast_and_fusion.16
  48.1 0.5 broadcast_and_fusion.18
  48.6 125.3 %all-reduce.22.cloned.1.call-done = bf16[80,8192]{1,0:T(8,128)(2,1)} async-done(((bf16[80,8192]{1,0:T(8,128)(2,1)}), bf16[80,8192]{1,0:T(8,128)(2,1)}) %all-reduce.22.cloned.1.call-update) | async-done | bytes 1310736 | tf_op jit(solution)/shard_map/psum | solution.py:68
  173.9 2.6 multiply_reduce_fusion
  176.5 30.2 %psum.183 = f32[]{:T(128)} all-reduce(f32[]{:T(128)} %get-tuple-element.50), channel_id=1, replica_groups=mesh['section'=16,'dp'=32] {'section'}, use_global_device_ids=true, to_apply=%region_2.3 | all-reduce | flops 1 | bytes 8 | tf_op jit(solution)/shard_map/psum | solution.py:70
  207.4 1.1 fusion.36
  208.6 0.0 copy-done
  208.6 0.0 copy-done.1
  208.6 2.9 fusion.25
  211.4 0.0 copy-start.2
  211.4 0.0 copy-start.3
  211.5 0.8 broadcast_select_fusion
  212.2 0.8 broadcast_select_fusion.9
  213.0 0.9 broadcast_select_fusion.8
  213.9 0.0 all-reduce.24.cloned.1.call-update
  214.0 0.0 all-reduce.26.cloned.1.call-start
  214.0 1.0 broadcast_select_fusion.1
  215.0 0.0 all-reduce.26.cloned.1.call-update
  215.1 0.0 copy-done.2
  215.1 0.0 copy-done.3
  215.1 1.0 fusion.26
  216.1 150.9 %all-reduce.24.cloned.1.call-done = (bf16[1,8192]{1,0:T(2,128)(2,1)}, bf16[1,8192]{1,0:T(2,128)(2,1)}, bf16[1,8192]{1,0:T(2,128)(2,1)}, bf16[1,8192]{1,0:T(2,128...) async-done(((bf16[1,8192]{1,0:T(2,128)(2,1)}, ...) | async-done | bytes 262160 | tf_op jit(solution)/shard_map/psum | solution.py:20
  367.0 165.0 %all-reduce.26.cloned.1.call-done = (bf16[8,8192]{1,0:T(8,128)(2,1)}, bf16[8,8192]{1,0:T(8,128)(2,1)}, bf16[8,8192]{1,0:T(8,128)(2,1)}, bf16[8,8192]{1,0:T(8,128...) async-done(((bf16[8,8192]{1,0:T(8,128)(2,1)}, bf16[8,8192]{1,0:T(8,128)(2,1)}, ...) | async-done | bytes 1048592 | tf_op jit(solution)/shard_map/psum | solution.py:20
  532.0 35.1 %concatenate.3 = bf16[80,8192]{1,0:T(8,128)(2,1)} concatenate(bf16[8,8192]{1,0:T(8,128)(2,1)} %get-tuple-element.21, bf16[1,8192]{1,0:T(2,128)(2,1)} %get-tuple-element.5, bf16[1,8192]{1,0:T(2,128)(2,1)} %get-tuple-element.6, bf16[8,8192]{1,0:T(8,128)(2,1)} %get-tuple-element.22, bf16[1,8192]{1,0:T(2,128)(2,1)} %get-tuple-element.7, bf16[1,8192]{1,0:T(2,128)(2,1)} %get-tuple-element.8, ...), dimensions={0} | concatenate | bytes 2621440 | tf_op jit(solution)/shard_map/concatenate | solution.py:86
  (3 shorter events, 0.1 us)
Async XLA Ops:
  7.2 166.8 %all-reduce.22.cloned.1.call-start = ((), (), s32[]{:S(2)}) async-start(), calls=%async_computation | async-start | bytes 2621440 | tf_op jit(solution)/shard_map/psum | solution.py:68
  7.9 359.1 %all-reduce.24.cloned.1.call-start = ((), (), s32[]{:S(2)}) async-start(), calls=%async_computation.1 | async-start | bytes 1048576 | tf_op jit(solution)/shard_map/psum | solution.py:20
  22.3 186.3 %copy-start = (f32[1,1,8,8192]{3,2,1,0:T(8,128)S(1)}, f32[1,1,8,8192]{3,2,1,0:T(8,128)}, u32[]{:S(2)}) copy-start(f32[1,1,8,8192]{3,2,1,0:T(8,128)} %param.8) | copy-start | bytes 786436
  22.3 186.3 %copy-start.1 = (f32[1,1,8,8192]{3,2,1,0:T(8,128)S(1)}, f32[1,1,8,8192]{3,2,1,0:T(8,128)}, u32[]{:S(2)}) copy-start(f32[1,1,8,8192]{3,2,1,0:T(8,128)} %param.10) | copy-start | bytes 786436
  211.4 3.6 copy-start.2
  211.4 3.6 copy-start.3
  214.0 318.0 %all-reduce.26.cloned.1.call-start = ((), (), s32[]{:S(2)}) async-start(), calls=%async_computation.2 | async-start | bytes 2097152 | tf_op jit(solution)/shard_map/psum | solution.py:20
Sparse Core Ops, SparseCore 0:
  11.5 162.4 all-reduce.21
  214.1 152.8 all-reduce.23
  371.9 160.0 all-reduce.25
where the time goes:
time: 578 us; the launch traced here: 574 us
  waiting for transfers between devices  442 us (76%)
  between operations  45.2 us (8%)
  local copies, waits for them, and re-layouts  39.7 us (7%)
  blocking collectives  30.2 us (5%)
  other arithmetic  16.4 us (3%)
    psum x2, waiting for transfers between devices, spread(): return lax.psum(jnp.where(mine, array, jnp.zeros_like(array)), axis)  316 us
    psum x1, waiting for transfers between devices, local(): total = lax.psum(flat.astype(jnp.bfloat16), 'dp').astype(jnp.float32)  125 us
    concatenate x1, local copies, waits for them, and re-layouts, local(): weights = jnp.concatenate(pieces, axis=0)  35.1 us
    psum x1, blocking collectives, local(): squares = lax.psum(jnp.sum(mean * mean), 'section')  30.2 us
  transfers between devices with their start and end apart: 3, of which 3 were waited for; matrix products, arithmetic and copies ran while one was open for 2% of the time, Pallas kernels for 0%

commit v1 on v0

v1 whole, which is shorter than its diff:
```python
import functools

import jax
import jax.numpy as jnp
from jax import lax
from jax.experimental import pallas as pl
from jax.experimental.pallas import tpu as pltpu
from jax.sharding import PartitionSpec as P

STEP = 10

beta_one = 0.9
beta_two = 0.95
epsilon = 1e-08
learn_rate = 0.0003
decay_rate = 0.1
average_keep = 0.999
clip_level = 0.5

XS = 4
YS = 8
CORES = 2


def tensor_layout(all_rows, slot_rows, layers):
    layer_rows = all_rows // layers
    kv_rows = (layer_rows - 2 - 2 * slot_rows) // 2
    counts = [slot_rows, kv_rows, kv_rows, slot_rows, 1, 1]
    layout = []
    start = 0
    for layer in range(layers):
        for position, count in enumerate(counts):
            layout.append((start, count, 1.0 if position < 4 else 0.0))
            start = start + count
    return layout


def adamw_moments(grad, moment, second, factor):
    clipped = factor * grad
    moment_new = beta_one * moment + (1.0 - beta_one) * clipped
    second_new = beta_two * second + (1.0 - beta_two) * clipped * clipped
    return moment_new, second_new


def adamw_master(master, moment_new, second_new, decay):
    direction = (
        moment_new
        / (1.0 - beta_one**STEP)
        / (jnp.sqrt(second_new / (1.0 - beta_two**STEP)) + epsilon)
    )
    return master - learn_rate * (direction + decay_rate * decay * master)


def clip_factor(squares, numel):
    return jnp.minimum(1.0, clip_level / jnp.sqrt(squares / numel + 1e-06))


def split_kernel(layout, replicas, owner, parts, master, moment, second, mean, payload):
    rows, width = mean.shape
    total = parts[0].astype(jnp.float32)
    for part in range(1, parts.shape[0]):
        total = total + parts[part].astype(jnp.float32)
    own = total / replicas
    mean[...] = own
    squared = own * own
    partial = squared[0:8]
    for row in range(8, rows, 8):
        partial = partial + squared[row : row + 8]
    partial = partial[:, :128] + partial[:, 128:]
    high = partial.astype(jnp.bfloat16)
    low = (partial - high.astype(jnp.float32)).astype(jnp.bfloat16)
    squares = jnp.concatenate(
        [high.astype(jnp.float32), low.astype(jnp.float32)], axis=1
    )
    zeros = jnp.zeros((8, width), jnp.float32)
    empty = jnp.concatenate([zeros, squares], axis=0).astype(jnp.bfloat16)
    for device in range(replicas):
        columns = slice(device * width, (device + 1) * width)
        payload[device, 0:16, :] = empty
        payload[device, 16:32, :] = jnp.concatenate(
            [moment[:, columns], second[:, columns]], axis=0
        ).astype(jnp.bfloat16)
        whole = master[:, columns]
        top = whole.astype(jnp.bfloat16).astype(jnp.float32)
        payload[device, 32:48, :] = jnp.concatenate(
            [top, whole - top], axis=0
        ).astype(jnp.bfloat16)
    for tensor, (start, count, flag) in enumerate(layout):
        block = mean[start : start + count, :]
        if count < 8:
            block = jnp.concatenate(
                [block, jnp.zeros((8 - count, width), jnp.float32)], axis=0
            )
        payload[owner[tensor], 0:16, :] = jnp.concatenate(
            [block, squares], axis=0
        ).astype(jnp.bfloat16)


def column_kernel(layout, numel, owner, squares, mean, received, copies, master, moment, second, decay):
    factor = clip_factor(jnp.sum(squares[...]), numel)
    for tensor, (start, count, flag) in enumerate(layout):
        root = owner[tensor]
        slots = received[root, 16:32, :].astype(jnp.float32)
        halves = received[root, 32:48, :].astype(jnp.float32)
        rows = slice(start, start + count)
        moment[rows, :] = slots[:count]
        second[rows, :] = slots[8 : 8 + count]
        master[rows, :] = halves[:count] + halves[8 : 8 + count]
        decay[rows, :] = jnp.full((count, decay.shape[1]), flag, jnp.float32)
    moment_new, second_new = adamw_moments(mean[...], moment[...], second[...], factor)
    weights = adamw_master(master[...], moment_new, second_new, decay[...])
    weights = weights.astype(jnp.bfloat16)
    for copy in range(copies.shape[0]):
        copies[copy] = weights


def owner_kernel(
    layout, numel, owner, me, squares, received, master, moment, second, average,
    master_out, moment_out, second_out, average_out,
):
    factor = clip_factor(jnp.sum(squares[...]), numel)
    count = jnp.int32(0)
    flag = jnp.float32(0.0)
    for tensor, (start, rows, decay) in enumerate(layout):
        mine = owner[tensor] == me[0]
        count = jnp.where(mine, rows, count)
        flag = jnp.where(mine, decay, flag)
    width = received.shape[2]
    used = lax.broadcasted_iota(jnp.int32, (8, width), 0) < count
    for source in range(received.shape[0]):
        columns = slice(source * width, (source + 1) * width)
        grad = received[source, 0:16, :].astype(jnp.float32)[0:8]
        olds = (master[:, columns], moment[:, columns], second[:, columns], average[:, columns])
        moment_new, second_new = adamw_moments(grad, olds[1], olds[2], factor)
        master_new = adamw_master(olds[0], moment_new, second_new, flag)
        average_new = average_keep * olds[3] + (1.0 - average_keep) * master_new
        master_out[:, columns] = jnp.where(used, master_new, olds[0])
        moment_out[:, columns] = jnp.where(used, moment_new, olds[1])
        second_out[:, columns] = jnp.where(used, second_new, olds[2])
        average_out[:, columns] = jnp.where(used, average_new, olds[3])


VMEM = pl.BlockSpec(memory_space=pltpu.VMEM)
SMEM = pl.BlockSpec(memory_space=pltpu.SMEM)
LIMIT = 32 * 1024 * 1024


def local(grads, owners, master, moment, second, average):
    rows = grads.shape[2]
    width = grads.shape[3]
    layout = tensor_layout(rows, master.shape[2], owners.shape[1] // 6)
    replicas = lax.axis_size("dp")
    sections = lax.axis_size("section")
    numel = sections * rows * width
    owner = owners[0]
    own_index = lax.axis_index("dp").astype(jnp.int32).reshape(1)
    along_x = [[x * YS + y for x in range(XS)] for y in range(YS)]
    along_y = [[x * YS + y for y in range(YS)] for x in range(XS)]
    along_z = [list(range(core, sections, CORES)) for core in range(CORES)]
    pairs = [[z * CORES + core for core in range(CORES)] for z in range(sections // CORES)]
    exchange = functools.partial(lax.all_to_all, split_axis=0, concat_axis=0, tiled=True)
    params = pltpu.CompilerParams(vmem_limit_bytes=LIMIT)
    olds = (master[0, 0], moment[0, 0], second[0, 0], average[0, 0])
    narrow = width // replicas
    wide = width // XS

    with jax.named_scope("reduce_x"):
        blocks = grads[0, 0].reshape(rows, XS, wide).transpose(1, 0, 2)
        blocks = exchange(blocks, "dp", axis_index_groups=along_x)
        summed = jnp.sum(blocks.astype(jnp.float32), axis=0).astype(jnp.bfloat16)
    with jax.named_scope("reduce_y"):
        blocks = summed.reshape(rows, YS, narrow).transpose(1, 0, 2)
        blocks = exchange(blocks, "dp", axis_index_groups=along_y)
    with jax.named_scope("split"):
        mean, payload = pl.pallas_call(
            functools.partial(split_kernel, layout, replicas),
            out_shape=(
                jax.ShapeDtypeStruct((rows, narrow), jnp.float32),
                jax.ShapeDtypeStruct((replicas, 48, narrow), jnp.bfloat16),
            ),
            in_specs=[SMEM, VMEM, VMEM, VMEM, VMEM],
            out_specs=(VMEM, VMEM),
            compiler_params=params,
        )(owner, blocks, olds[0], olds[1], olds[2])
    with jax.named_scope("to_owners"):
        received = exchange(payload, "dp")
    with jax.named_scope("squares"):
        squares = jnp.sum(received[:, 8:16, :].astype(jnp.float32), axis=0)
        squares = squares[:, :128] + squares[:, 128:]
        squares = jnp.broadcast_to(squares, (sections // CORES,) + squares.shape)
        squares = exchange(squares, "section", axis_index_groups=along_z)
        squares = lax.all_gather(squares, "section", axis_index_groups=pairs, tiled=True)
    with jax.named_scope("columns"):
        copies = pl.pallas_call(
            functools.partial(column_kernel, layout, numel),
            out_shape=jax.ShapeDtypeStruct((YS, rows, narrow), jnp.bfloat16),
            in_specs=[SMEM, VMEM, VMEM, VMEM],
            out_specs=VMEM,
            scratch_shapes=[pltpu.VMEM((rows, narrow), jnp.float32)] * 4,
            compiler_params=params,
        )(owner, squares, mean, received)
    with jax.named_scope("gather_y"):
        gathered = exchange(copies, "dp", axis_index_groups=along_y)
    with jax.named_scope("gather_x"):
        copies = jnp.broadcast_to(gathered, (XS,) + gathered.shape)
        gathered = exchange(copies, "dp", axis_index_groups=along_x)
        weights = gathered.transpose(2, 0, 1, 3).reshape(rows, width)
    with jax.named_scope("owned"):
        state = jax.ShapeDtypeStruct(olds[0].shape, jnp.float32)
        news = pl.pallas_call(
            functools.partial(owner_kernel, layout, numel),
            out_shape=(state,) * 4,
            in_specs=[SMEM, SMEM] + [VMEM] * 6,
            out_specs=(VMEM,) * 4,
            compiler_params=params,
        )(owner, own_index, squares, received, *olds)
    return (weights[None],) + tuple(new[None, None] for new in news)


def solution(mesh):
    in_specs = (
        P("section", "dp", None, None),
        P("section", None),
        P("section", "dp", None, None),
        P("section", "dp", None, None),
        P("section", "dp", None, None),
        P("section", "dp", None, None),
    )
    out_specs = (
        P("section", None, None),
        P("section", "dp", None, None),
        P("section", "dp", None, None),
        P("section", "dp", None, None),
        P("section", "dp", None, None),
    )
    return jax.shard_map(local, mesh=mesh, in_specs=in_specs, out_specs=out_specs, check_vma=False)
```

time: 578 us -> 135 us (0.23)
  waiting for transfers between devices: 442 us -> 14.5 us
  blocking collectives: 30.2 us -> 102 us
  between operations: 45.2 us -> 0.72 us
  local copies, waits for them, and re-layouts: 39.7 us -> 9.74 us
  other arithmetic: 16.4 us -> 0.27 us
    psum x3 -> x0, waiting for transfers between devices: 441 us -> none  [the longest x2 316 us: spread(): return lax.psum(jnp.where(mine, array, jnp.zeros_like(array)), axis)]
    all_to_all x0 -> x5, blocking collectives: none -> 92.2 us  [the longest x1 21.2 us: local(): received = exchange(payload, 'dp')]
    concatenate x1 -> x0, local copies, waits for them, and re-layouts: 35.1 us -> none  [local(): weights = jnp.concatenate(pieces, axis=0)]
    psum x1 -> x0, blocking collectives: 30.2 us -> none  [local(): squares = lax.psum(jnp.sum(mean * mean), 'section')]
    all_to_all x0 -> x1, waiting for transfers between devices: none -> 14.5 us  [local(): gathered = exchange(copies, 'dp', axis_index_groups=along_x)]
    all_gather x0 -> x1, blocking collectives: none -> 10 us  [local(): lax.all_gather(squares, 'section', axis_index_groups=pairs, tiled=True)]
    and x12 -> x0, other arithmetic: 6.34 us -> none  [local(): marks = jnp.logical_and(slot_ids < count, owner[tensor] == own_index)]
  transfers between devices with their start and end apart: 3 -> 1, of which waited for: 3 -> 1; matrix products, arithmetic and copies ran while one was open for 2% -> 0% of each run, Pallas kernels for 0% -> 1%
where the time goes in v1:
time: 135 us
  blocking collectives  102 us (76%)
  waiting for transfers between devices  14.5 us (11%)
  local copies, waits for them, and re-layouts  9.74 us (7%)
  starting transfers between devices  3.67 us (3%)
  Pallas kernels  3.43 us (3%)
    all_to_all x1, blocking collectives, local(): received = exchange(payload, 'dp')  21.2 us
    all_to_all x1, blocking collectives, local(): blocks = exchange(blocks, 'dp', axis_index_groups=along_y)  20.3 us
    all_to_all x1, blocking collectives, local(): blocks = exchange(blocks, 'dp', axis_index_groups=along_x)  17.9 us
    all_to_all x1, blocking collectives, local(): squares = exchange(squares, 'section', axis_index_groups=along_z)  16.7 us
    all_to_all x1, blocking collectives, local(): gathered = exchange(copies, 'dp', axis_index_groups=along_y)  16.1 us
    all_to_all x1, waiting for transfers between devices, local(): gathered = exchange(copies, 'dp', axis_index_groups=along_x)  14.5 us
    all_gather x1, blocking collectives, local(): lax.all_gather(squares, 'section', axis_index_groups=pairs, tiled=True)  10 us
    all_to_all x1, starting transfers between devices, local(): gathered = exchange(copies, 'dp', axis_index_groups=along_x)  3.67 us
  transfers between devices with their start and end apart: 1, of which 1 were waited for; matrix products, arithmetic and copies ran while one was open for 0% of the time, Pallas kernels for 1%

profile of v1, /device:TPU:1, one launch (start us, length us, event | category | flops | bytes accessed | tf_op | source)
XLA Modules:
  0.0 134.6 jit_solution(10834925007156951539)
XLA Ops:
  0.6 3.2 %squeeze.19 = bf16[80,4,2048]{2,1,0:T(4,128)(2,1)S(1)} reshape(bf16[1,1,80,8192]{3,2,1,0:T(8,128)(2,1)} %param.6) | data formatting | bytes 2621440 | tf_op jit(solution)/shard_map/reduce_x/reshape;reduce_x/squeeze | solution.py:168
  3.9 0.7 copy.16
  4.6 17.9 %all_to_all.30 = bf16[4,80,2048]{2,1,0:T(8,128)(2,1)S(1)} all-to-all(bf16[4,80,2048]{2,1,0:T(8,128)(2,1)S(1)} %copy.16), channel_id=1, replica_groups={{0,8,16,24},{1,9,17,25},{2,10,18,26},{3,11,19,27},{4,12,20,28},{5,13,21..., dimensions={0} | all-to-all | bytes 2621440 | tf_op jit(solution)/shard_map/reduce_x/all_to_all | solution.py:169
  22.5 0.0 copy-start
  22.5 0.0 copy-start.1
  22.5 0.0 copy-start.2
  22.5 0.0 copy-start.4
  22.5 0.2 reduce_sum.21
  22.8 20.3 %all_to_all.31.parts = bf16[8,80,256]{2,1,0:T(8,128)(2,1)S(1)} all-to-all(bf16[8,80,256]{2,1,0:T(8,128)(2,1)S(1)} %bitcast.35), channel_id=1, replica_groups={{0,1,2,3,4,5,6,7},{8,9,10,11,12,13,14,15},{16,17,18,19,20,21,22,23},{24..., dimensions={0} | all-to-all | bytes 655360 | tf_op jit(solution)/shard_map/reduce_y/all_to_all | solution.py:173
  43.1 0.0 copy-done
  43.1 0.0 copy-done.1
  43.1 0.0 copy-done.2
  43.1 0.0 copy-done.4
  43.1 0.7 split.1
  43.7 21.2 %all_to_all.32.received = bf16[32,48,256]{2,1,0:T(8,128)(2,1)S(1)} all-to-all(bf16[32,48,256]{2,1,0:T(8,128)(2,1)S(1)} %get-tuple-element.11), channel_id=1, replica_groups=mesh['section'=16,'dp'=32] {'dp'}, dimensions={0} | all-to-all | bytes 1572864 | tf_op jit(solution)/shard_map/to_owners/all_to_all | solution.py:186
  65.0 16.7 %all_to_all.33 = f32[8,8,128]{2,1,0:T(8,128)S(1)} all-to-all(f32[8,8,128]{2,1,0:T(8,128)S(1)} %broadcast_in_dim.18), channel_id=1, replica_groups={{0,64,128,192,256,320,384,448},{32,96,160,224,288,352,416,480},{1,65,12..., dimensions={0} | all-to-all | bytes 65536 | tf_op jit(solution)/shard_map/squares/all_to_all | solution.py:191
  81.7 10.0 %all_gather.3.squares = f32[16,8,128]{2,1,0:T(8,128)S(1)} all-gather(f32[8,8,128]{2,1,0:T(8,128)S(1)} %all_to_all.33), channel_id=1, replica_groups={{0,32},{64,96},{128,160},{192,224},{256,288},{320,352},{384,416},{448,4..., dimensions={0}, use_global_device_ids=true | all-gather | bytes 98304 | tf_op jit(solution)/shard_map/squares/all_gather | solution.py:192
  91.7 0.8 columns.1
  92.6 16.1 %all_to_all.34 = bf16[8,80,256]{2,1,0:T(8,128)(2,1)S(1)} all-to-all(bf16[8,80,256]{2,1,0:T(8,128)(2,1)S(1)} %columns.1), channel_id=1, replica_groups={{0,1,2,3,4,5,6,7},{8,9,10,11,12,13,14,15},{16,17,18,19,20,21,22,23},{24..., dimensions={0} | all-to-all | bytes 655360 | tf_op jit(solution)/shard_map/gather_y/all_to_all | solution.py:203
  108.7 0.1 copy.18
  108.8 1.1 broadcast_in_dim.19
  109.9 0.0 copy-start.3
  110.0 3.7 %all-to-all-start.5 = ((bf16[4,8,80,256]{3,1,2,0:T(8,128)(2,1)}), bf16[4,8,80,256]{3,1,2,0:T(8,128)(2,1)S(1)}, u32[]{:S(2)}, u32[]{:S(2)}) async-start(bf16[4,8,80,256]{3,1,2,0:T(8,128)(2,1)} %broadcast_in_dim.19), calls=%async_computation.5 | async-start | bytes 2621440 | tf_op jit(solution)/shard_map/gather_x/all_to_all | solution.py:206
  113.6 0.0 copy-done.3
  113.6 1.9 %owned.1 = (f32[8,8192]{1,0:T(8,128)}, f32[8,8192]{1,0:T(8,128)}, f32[8,8192]{1,0:T(8,128)}, f32[8,8192]{1,0:T(8,128)}) custom-call(s32[24]{0:T(128)S(1)} %bitcast.32, s32[1]{0:T(128)} %bitcast.7.me, f32[16,8,128]{2,1,0:T(8,128)S(1)} %all_gather.3.squares, bf16[32,48,256]{2,1,0:T(8,128)(2,1)S(1)} %all_to_all.32.received, f32[8,8192]{1,0:T(8,128)S(1)} %bitcast.24, ...), custom_call_target="tpu_custom_call" | custom-call | tf_op jit(solution)/shard_map/owned/pallas_call | solution.py:210
  115.6 14.5 %all-to-all-done.5 = bf16[4,8,80,256]{3,1,2,0:T(8,128)(2,1)S(1)} async-done(((bf16[4,8,80,256]{3,1,2,0:T(8,128)(2,1)}), bf16[4,8,80,256]{3,1,2,0:T(8,128)(2,1)S(1)}, u32[]{:S(2)}, u32[]{:S(2)}) %all-to-all-start.5) | async-done | bytes 1310752 | tf_op jit(solution)/shard_map/gather_x/all_to_all | solution.py:206
  130.1 1.2 copy.19
  131.3 3.3 %reshape.20 = bf16[1,80,8192]{2,1,0:T(8,128)(2,1)} reshape(bf16[80,4,8,256]{3,2,1,0:T(8,128)(2,1)} %copy.19) | data formatting | bytes 2621440 | tf_op jit(solution)/shard_map/broadcast_in_dim;gather_x/reshape | solution.py:217
  (4 shorter events, 0.1 us)
Async XLA Ops:
  22.5 20.6 %copy-start = (f32[1,1,8,8192]{3,2,1,0:T(8,128)S(1)}, f32[1,1,8,8192]{3,2,1,0:T(8,128)}, u32[]{:S(2)}) copy-start(f32[1,1,8,8192]{3,2,1,0:T(8,128)} %param.8) | copy-start | bytes 786436
  22.5 20.6 %copy-start.1 = (f32[1,1,8,8192]{3,2,1,0:T(8,128)S(1)}, f32[1,1,8,8192]{3,2,1,0:T(8,128)}, u32[]{:S(2)}) copy-start(f32[1,1,8,8192]{3,2,1,0:T(8,128)} %param.9) | copy-start | bytes 786436
  22.5 20.6 %copy-start.2 = (f32[1,1,8,8192]{3,2,1,0:T(8,128)S(1)}, f32[1,1,8,8192]{3,2,1,0:T(8,128)}, u32[]{:S(2)}) copy-start(f32[1,1,8,8192]{3,2,1,0:T(8,128)} %param.10) | copy-start | bytes 786436
  22.5 20.6 %copy-start.4 = (s32[1,24]{1,0:T(1,128)S(1)}, s32[1,24]{1,0:T(1,128)}, u32[]{:S(2)}) copy-start(s32[1,24]{1,0:T(1,128)} %param.7) | copy-start | bytes 292
  109.9 3.7 %copy-start.3 = (f32[1,1,8,8192]{3,2,1,0:T(8,128)S(1)}, f32[1,1,8,8192]{3,2,1,0:T(8,128)}, u32[]{:S(2)}) copy-start(f32[1,1,8,8192]{3,2,1,0:T(8,128)} %param.11) | copy-start | bytes 786436
  110.0 20.2 %all-to-all-start.5 = ((bf16[4,8,80,256]{3,1,2,0:T(8,128)(2,1)}), bf16[4,8,80,256]{3,1,2,0:T(8,128)(2,1)S(1)}, u32[]{:S(2)}, u32[]{:S(2)}) async-start(bf16[4,8,80,256]{3,1,2,0:T(8,128)(2,1)} %broadcast_in_dim.19), calls=%async_computation.5 | async-start | bytes 2621440 | tf_op jit(solution)/shard_map/gather_x/all_to_all | solution.py:206

commit v2 on v1

--- a/solution.py
+++ b/solution.py
@@ -140,7 +140,41 @@
         average_out[:, columns] = jnp.where(used, average_new, olds[3])
 
 
+def cut_kernel(grads, blocks, sems):
+    parts, _, width = blocks.shape
+    moves = [
+        pltpu.make_async_copy(
+            grads.at[0, 0, :, pl.ds(part * width, width)], blocks.at[part], sems.at[part]
+        )
+        for part in range(parts)
+    ]
+    for move in moves:
+        move.start()
+    for move in moves:
+        move.wait()
+
+
+def copies_kernel(block, copies):
+    for copy in range(copies.shape[0]):
+        copies[copy] = block[...]
+
+
+def join_kernel(blocks, weights, sems):
+    parts, _, width = blocks.shape
+    moves = [
+        pltpu.make_async_copy(
+            blocks.at[part], weights.at[0, :, pl.ds(part * width, width)], sems.at[part]
+        )
+        for part in range(parts)
+    ]
+    for move in moves:
+        move.start()
+    for move in moves:
+        move.wait()
+
+
 VMEM = pl.BlockSpec(memory_space=pltpu.VMEM)
+HBM = pl.BlockSpec(memory_space=pltpu.HBM)
 SMEM = pl.BlockSpec(memory_space=pltpu.SMEM)
 LIMIT = 32 * 1024 * 1024
 
@@ -165,7 +199,14 @@
     wide = width // XS
 
     with jax.named_scope("reduce_x"):
-        blocks = grads[0, 0].reshape(rows, XS, wide).transpose(1, 0, 2)
+        blocks = pl.pallas_call(
+            cut_kernel,
+            out_shape=jax.ShapeDtypeStruct((XS, rows, wide), jnp.bfloat16),
+            in_specs=[HBM],
+            out_specs=VMEM,
+            scratch_shapes=[pltpu.SemaphoreType.DMA((XS,))],
+            compiler_params=pltpu.CompilerParams(vmem_limit_bytes=LIMIT),
+        )(grads)
         blocks = exchange(blocks, "dp", axis_index_groups=along_x)
         summed = jnp.sum(blocks.astype(jnp.float32), axis=0).astype(jnp.bfloat16)
     with jax.named_scope("reduce_y"):
@@ -202,9 +243,23 @@
     with jax.named_scope("gather_y"):
         gathered = exchange(copies, "dp", axis_index_groups=along_y)
     with jax.named_scope("gather_x"):
-        copies = jnp.broadcast_to(gathered, (XS,) + gathered.shape)
+        copies = pl.pallas_call(
+            copies_kernel,
+            out_shape=jax.ShapeDtypeStruct((XS,) + gathered.shape, jnp.bfloat16),
+            in_specs=[VMEM],
+            out_specs=VMEM,
+            compiler_params=params,
+        )(gathered)
         gathered = exchange(copies, "dp", axis_index_groups=along_x)
-        weights = gathered.transpose(2, 0, 1, 3).reshape(rows, width)
+    with jax.named_scope("join"):
+        weights = pl.pallas_call(
+            join_kernel,
+            out_shape=jax.ShapeDtypeStruct((1, rows, width), jnp.bfloat16),
+            in_specs=[VMEM],
+            out_specs=HBM,
+            scratch_shapes=[pltpu.SemaphoreType.DMA((replicas,))],
+            compiler_params=params,
+        )(gathered.reshape(replicas, rows, narrow))
     with jax.named_scope("owned"):
         state = jax.ShapeDtypeStruct(olds[0].shape, jnp.float32)
         news = pl.pallas_call(
@@ -214,7 +269,7 @@
             out_specs=(VMEM,) * 4,
             compiler_params=params,
         )(owner, own_index, squares, received, *olds)
-    return (weights[None],) + tuple(new[None, None] for new in news)
+    return (weights,) + tuple(new[None, None] for new in news)
 
 
 def solution(mesh):

time: 135 us -> 129 us (0.956)
  local copies, waits for them, and re-layouts: 9.74 us -> 1.36 us
  Pallas kernels: 3.43 us -> 6 us
    reshape x1 -> x0, local copies, waits for them, and re-layouts: 3.27 us -> none  [local(): return (weights[None],) + tuple((new[None, None] for new in news))]
    squeeze x1 -> x0, local copies, waits for them, and re-layouts: 3.23 us -> none  [local(): blocks = grads[0, 0].reshape(rows, XS, wide).transpose(1, 0, 2)]
    pallas_call x0 -> x3, Pallas kernels: none -> 2.58 us  [the longest x1 1.31 us: local(): pl.pallas_call(join_kernel, out_shape=jax.ShapeDtypeStruct((1, rows, widt...]
    transpose x2 -> x0, local copies, waits for them, and re-layouts: 1.96 us -> none  [the longest x1 1.24 us: local(): weights = gathered.transpose(2, 0, 1, 3).reshape(rows, width)]
where the time goes in v2:
time: 129 us
  blocking collectives  102 us (79%)
  waiting for transfers between devices  14.5 us (11%)
  Pallas kernels  6 us (5%)
  starting transfers between devices  3.67 us (3%)
  local copies, waits for them, and re-layouts  1.36 us (1%)
    all_to_all x1, blocking collectives, local(): received = exchange(payload, 'dp')  21.2 us
    all_to_all x1, blocking collectives, local(): blocks = exchange(blocks, 'dp', axis_index_groups=along_y)  20.3 us
    all_to_all x1, blocking collectives, local(): blocks = exchange(blocks, 'dp', axis_index_groups=along_x)  17.9 us
    all_to_all x1, blocking collectives, local(): squares = exchange(squares, 'section', axis_index_groups=along_z)  16.7 us
    all_to_all x1, blocking collectives, local(): gathered = exchange(copies, 'dp', axis_index_groups=along_y)  16.1 us
    all_to_all x1, waiting for transfers between devices, local(): gathered = exchange(copies, 'dp', axis_index_groups=along_x)  14.5 us
    all_gather x1, blocking collectives, local(): lax.all_gather(squares, 'section', axis_index_groups=pairs, tiled=True)  10 us
    all_to_all x1, starting transfers between devices, local(): gathered = exchange(copies, 'dp', axis_index_groups=along_x)  3.67 us
  transfers between devices with their start and end apart: 1, of which 1 were waited for; matrix products, arithmetic and copies ran while one was open for 0% of the time, Pallas kernels for 1%

profile of v2, /device:TPU:1, one launch (start us, length us, event | category | flops | bytes accessed | tf_op | source)
XLA Modules:
  0.0 128.8 jit_solution(6127841640407680914)
XLA Ops:
  0.6 0.0 copy-start
  0.6 1.3 %copy-done = bf16[1,1,80,8192]{3,2,1,0:T(8,128)(2,1)S(1)} copy-done((bf16[1,1,80,8192]{3,2,1,0:T(8,128)(2,1)S(1)}, bf16[1,1,80,8192]{3,2,1,0:T(8,128)(2,1)}, u32[]{:S(2)}) %copy-start) | copy-done | bytes 1310744
  1.9 0.1 reduce_x.1
  2.1 17.9 %all_to_all.30 = bf16[4,80,2048]{2,1,0:T(8,128)(2,1)S(1)} all-to-all(bf16[4,80,2048]{2,1,0:T(8,128)(2,1)S(1)} %reduce_x.1), channel_id=1, replica_groups={{0,8,16,24},{1,9,17,25},{2,10,18,26},{3,11,19,27},{4,12,20,28},{5,13,21..., dimensions={0} | all-to-all | bytes 2621440 | tf_op jit(solution)/shard_map/reduce_x/all_to_all | solution.py:210
  20.0 0.0 copy-start.1
  20.0 0.0 copy-start.2
  20.0 0.0 copy-start.3
  20.0 0.0 copy-start.5
  20.0 0.2 reduce_sum.21
  20.3 20.3 %all_to_all.31.parts = bf16[8,80,256]{2,1,0:T(8,128)(2,1)S(1)} all-to-all(bf16[8,80,256]{2,1,0:T(8,128)(2,1)S(1)} %bitcast.29), channel_id=1, replica_groups={{0,1,2,3,4,5,6,7},{8,9,10,11,12,13,14,15},{16,17,18,19,20,21,22,23},{24..., dimensions={0} | all-to-all | bytes 655360 | tf_op jit(solution)/shard_map/reduce_y/all_to_all | solution.py:214
  40.6 0.0 copy-done.1
  40.6 0.0 copy-done.2
  40.6 0.0 copy-done.3
  40.6 0.0 copy-done.5
  40.6 0.7 split.1
  41.2 21.2 %all_to_all.32.received = bf16[32,48,256]{2,1,0:T(8,128)(2,1)S(1)} all-to-all(bf16[32,48,256]{2,1,0:T(8,128)(2,1)S(1)} %get-tuple-element.11), channel_id=1, replica_groups=mesh['section'=16,'dp'=32] {'dp'}, dimensions={0} | all-to-all | bytes 1572864 | tf_op jit(solution)/shard_map/to_owners/all_to_all | solution.py:227
  62.5 16.7 %all_to_all.33 = f32[8,8,128]{2,1,0:T(8,128)S(1)} all-to-all(f32[8,8,128]{2,1,0:T(8,128)S(1)} %broadcast_in_dim.15), channel_id=1, replica_groups={{0,64,128,192,256,320,384,448},{32,96,160,224,288,352,416,480},{1,65,12..., dimensions={0} | all-to-all | bytes 65536 | tf_op jit(solution)/shard_map/squares/all_to_all | solution.py:232
  79.2 10.0 %all_gather.3.squares = f32[16,8,128]{2,1,0:T(8,128)S(1)} all-gather(f32[8,8,128]{2,1,0:T(8,128)S(1)} %all_to_all.33), channel_id=1, replica_groups={{0,32},{64,96},{128,160},{192,224},{256,288},{320,352},{384,416},{448,4..., dimensions={0}, use_global_device_ids=true | all-gather | bytes 98304 | tf_op jit(solution)/shard_map/squares/all_gather | solution.py:233
  89.2 0.8 columns.1
  90.1 16.1 %all_to_all.34.block = bf16[8,80,256]{2,1,0:T(8,128)(2,1)S(1)} all-to-all(bf16[8,80,256]{2,1,0:T(8,128)(2,1)S(1)} %columns.1), channel_id=1, replica_groups={{0,1,2,3,4,5,6,7},{8,9,10,11,12,13,14,15},{16,17,18,19,20,21,22,23},{24..., dimensions={0} | all-to-all | bytes 655360 | tf_op jit(solution)/shard_map/gather_y/all_to_all | solution.py:244
  106.2 1.1 gather_x.1
  107.3 0.0 copy-start.4
  107.3 3.7 %all-to-all-start.5 = ((bf16[4,8,80,256]{3,2,1,0:T(8,128)(2,1)}), bf16[4,8,80,256]{3,2,1,0:T(8,128)(2,1)S(1)}, u32[]{:S(2)}, u32[]{:S(2)}) async-start(bf16[4,8,80,256]{3,2,1,0:T(8,128)(2,1)} %gather_x.1), calls=%async_computation.5 | async-start | bytes 2621440 | tf_op jit(solution)/shard_map/gather_x/all_to_all | solution.py:253
  111.0 0.0 copy-done.4
  111.0 1.9 %owned.1 = (f32[8,8192]{1,0:T(8,128)}, f32[8,8192]{1,0:T(8,128)}, f32[8,8192]{1,0:T(8,128)}, f32[8,8192]{1,0:T(8,128)}) custom-call(s32[24]{0:T(128)S(1)} %bitcast.28, s32[1]{0:T(128)} %bitcast.6.me, f32[16,8,128]{2,1,0:T(8,128)S(1)} %all_gather.3.squares, bf16[32,48,256]{2,1,0:T(8,128)(2,1)S(1)} %all_to_all.32.received, f32[8,8192]{1,0:T(8,128)S(1)} %bitcast.20, ...), custom_call_target="tpu_custom_call" | custom-call | tf_op jit(solution)/shard_map/owned/pallas_call | solution.py:265
  112.9 14.5 %all-to-all-done.5 = bf16[4,8,80,256]{3,2,1,0:T(8,128)(2,1)S(1)} async-done(((bf16[4,8,80,256]{3,2,1,0:T(8,128)(2,1)}), bf16[4,8,80,256]{3,2,1,0:T(8,128)(2,1)S(1)}, u32[]{:S(2)}, u32[]{:S(2)}) %all-to-all-start.5) | async-done | bytes 1310752 | tf_op jit(solution)/shard_map/gather_x/all_to_all | solution.py:253
  127.5 1.3 %join.1 = bf16[1,80,8192]{2,1,0:T(8,128)(2,1)} custom-call(bf16[32,80,256]{2,1,0:T(8,128)(2,1)S(1)} %bitcast.18), custom_call_target="tpu_custom_call" | custom-call | tf_op jit(solution)/shard_map/join/pallas_call | solution.py:255
  (4 shorter events, 0.1 us)
Async XLA Ops:
  0.6 1.3 %copy-start = (bf16[1,1,80,8192]{3,2,1,0:T(8,128)(2,1)S(1)}, bf16[1,1,80,8192]{3,2,1,0:T(8,128)(2,1)}, u32[]{:S(2)}) copy-start(bf16[1,1,80,8192]{3,2,1,0:T(8,128)(2,1)} %grads.1) | copy-start | bytes 3932164
  20.0 20.6 %copy-start.1 = (f32[1,1,8,8192]{3,2,1,0:T(8,128)S(1)}, f32[1,1,8,8192]{3,2,1,0:T(8,128)}, u32[]{:S(2)}) copy-start(f32[1,1,8,8192]{3,2,1,0:T(8,128)} %param.8) | copy-start | bytes 786436
  20.0 20.6 %copy-start.2 = (f32[1,1,8,8192]{3,2,1,0:T(8,128)S(1)}, f32[1,1,8,8192]{3,2,1,0:T(8,128)}, u32[]{:S(2)}) copy-start(f32[1,1,8,8192]{3,2,1,0:T(8,128)} %param.9) | copy-start | bytes 786436
  20.0 20.6 %copy-start.3 = (f32[1,1,8,8192]{3,2,1,0:T(8,128)S(1)}, f32[1,1,8,8192]{3,2,1,0:T(8,128)}, u32[]{:S(2)}) copy-start(f32[1,1,8,8192]{3,2,1,0:T(8,128)} %param.10) | copy-start | bytes 786436
  20.0 20.6 %copy-start.5 = (s32[1,24]{1,0:T(1,128)S(1)}, s32[1,24]{1,0:T(1,128)}, u32[]{:S(2)}) copy-start(s32[1,24]{1,0:T(1,128)} %param.7) | copy-start | bytes 292
  107.3 3.7 %copy-start.4 = (f32[1,1,8,8192]{3,2,1,0:T(8,128)S(1)}, f32[1,1,8,8192]{3,2,1,0:T(8,128)}, u32[]{:S(2)}) copy-start(f32[1,1,8,8192]{3,2,1,0:T(8,128)} %param.11) | copy-start | bytes 786436
  107.3 20.2 %all-to-all-start.5 = ((bf16[4,8,80,256]{3,2,1,0:T(8,128)(2,1)}), bf16[4,8,80,256]{3,2,1,0:T(8,128)(2,1)S(1)}, u32[]{:S(2)}, u32[]{:S(2)}) async-start(bf16[4,8,80,256]{3,2,1,0:T(8,128)(2,1)} %gather_x.1), calls=%async_computation.5 | async-start | bytes 2621440 | tf_op jit(solution)/shard_map/gather_x/all_to_all | solution.py:253

commit v3 on v2

--- a/solution.py
+++ b/solution.py
@@ -57,6 +57,7 @@
 
 def split_kernel(layout, replicas, owner, parts, master, moment, second, mean, payload):
     rows, width = mean.shape
+    half = width // 2
     total = parts[0].astype(jnp.float32)
     for part in range(1, parts.shape[0]):
         total = total + parts[part].astype(jnp.float32)
@@ -66,25 +67,23 @@
     partial = squared[0:8]
     for row in range(8, rows, 8):
         partial = partial + squared[row : row + 8]
-    partial = partial[:, :128] + partial[:, 128:]
-    high = partial.astype(jnp.bfloat16)
-    low = (partial - high.astype(jnp.float32)).astype(jnp.bfloat16)
-    squares = jnp.concatenate(
-        [high.astype(jnp.float32), low.astype(jnp.float32)], axis=1
-    )
-    zeros = jnp.zeros((8, width), jnp.float32)
-    empty = jnp.concatenate([zeros, squares], axis=0).astype(jnp.bfloat16)
+    partial = partial[:, :half] + partial[:, half:]
+    partial = partial[0:4] + partial[4:8]
+    high = partial.astype(jnp.bfloat16).astype(jnp.float32)
+    squares = jnp.concatenate([high, partial - high], axis=0).astype(jnp.bfloat16)
+    empty = jnp.zeros((16, half), jnp.bfloat16)
     for device in range(replicas):
-        columns = slice(device * width, (device + 1) * width)
         payload[device, 0:16, :] = empty
-        payload[device, 16:32, :] = jnp.concatenate(
-            [moment[:, columns], second[:, columns]], axis=0
-        ).astype(jnp.bfloat16)
-        whole = master[:, columns]
-        top = whole.astype(jnp.bfloat16).astype(jnp.float32)
-        payload[device, 32:48, :] = jnp.concatenate(
-            [top, whole - top], axis=0
-        ).astype(jnp.bfloat16)
+        for place, state in enumerate((moment, second, master)):
+            block = jnp.concatenate(
+                [
+                    state[:, device * width : device * width + half],
+                    state[:, device * width + half : (device + 1) * width],
+                ],
+                axis=0,
+            )
+            payload[device, 16 * place + 16 : 16 * place + 32, :] = block.astype(jnp.bfloat16)
+        payload[device, 64:72, :] = squares
     for tensor, (start, count, flag) in enumerate(layout):
         block = mean[start : start + count, :]
         if count < 8:
@@ -92,20 +91,20 @@
                 [block, jnp.zeros((8 - count, width), jnp.float32)], axis=0
             )
         payload[owner[tensor], 0:16, :] = jnp.concatenate(
-            [block, squares], axis=0
+            [block[:, :half], block[:, half:]], axis=0
         ).astype(jnp.bfloat16)
 
 
 def column_kernel(layout, numel, owner, squares, mean, received, copies, master, moment, second, decay):
     factor = clip_factor(jnp.sum(squares[...]), numel)
+    half = mean.shape[1] // 2
     for tensor, (start, count, flag) in enumerate(layout):
         root = owner[tensor]
-        slots = received[root, 16:32, :].astype(jnp.float32)
-        halves = received[root, 32:48, :].astype(jnp.float32)
         rows = slice(start, start + count)
-        moment[rows, :] = slots[:count]
-        second[rows, :] = slots[8 : 8 + count]
-        master[rows, :] = halves[:count] + halves[8 : 8 + count]
+        for place, state in enumerate((moment, second, master)):
+            block = received[root, 16 * place + 16 : 16 * place + 32, :].astype(jnp.float32)
+            state[rows, :half] = block[:count]
+            state[rows, half:] = block[8 : 8 + count]
         decay[rows, :] = jnp.full((count, decay.shape[1]), flag, jnp.float32)
     moment_new, second_new = adamw_moments(mean[...], moment[...], second[...], factor)
     weights = adamw_master(master[...], moment_new, second_new, decay[...])
@@ -125,11 +124,12 @@
         mine = owner[tensor] == me[0]
         count = jnp.where(mine, rows, count)
         flag = jnp.where(mine, decay, flag)
-    width = received.shape[2]
+    width = 2 * received.shape[2]
     used = lax.broadcasted_iota(jnp.int32, (8, width), 0) < count
     for source in range(received.shape[0]):
         columns = slice(source * width, (source + 1) * width)
-        grad = received[source, 0:16, :].astype(jnp.float32)[0:8]
+        grad = received[source, 0:16, :].astype(jnp.float32)
+        grad = jnp.concatenate([grad[0:8], grad[8:16]], axis=1)
         olds = (master[:, columns], moment[:, columns], second[:, columns], average[:, columns])
         moment_new, second_new = adamw_moments(grad, olds[1], olds[2], factor)
         master_new = adamw_master(olds[0], moment_new, second_new, flag)
@@ -154,19 +154,20 @@
         move.wait()
 
 
-def copies_kernel(block, copies):
-    for copy in range(copies.shape[0]):
-        copies[copy] = block[...]
-
-
-def join_kernel(blocks, weights, sems):
-    parts, _, width = blocks.shape
-    moves = [
-        pltpu.make_async_copy(
-            blocks.at[part], weights.at[0, :, pl.ds(part * width, width)], sems.at[part]
-        )
-        for part in range(parts)
-    ]
+def join_kernel(me, *refs):
+    blocks, (weights, sems) = refs[:-2], refs[-2:]
+    count, _, width = blocks[0].shape
+    own = lax.div(me[0], count)
+    moves = []
+    for step, block in enumerate(blocks):
+        source = lax.rem(own + (len(blocks) - step), len(blocks))
+        for part in range(count):
+            start = pl.multiple_of((source * count + part) * width, width)
+            moves.append(
+                pltpu.make_async_copy(
+                    block.at[part], weights.at[0, :, pl.ds(start, width)], sems.at[step, part]
+                )
+            )
     for move in moves:
         move.start()
     for move in moves:
@@ -217,7 +218,7 @@
             functools.partial(split_kernel, layout, replicas),
             out_shape=(
                 jax.ShapeDtypeStruct((rows, narrow), jnp.float32),
-                jax.ShapeDtypeStruct((replicas, 48, narrow), jnp.bfloat16),
+                jax.ShapeDtypeStruct((replicas, 72, narrow // 2), jnp.bfloat16),
             ),
             in_specs=[SMEM, VMEM, VMEM, VMEM, VMEM],
             out_specs=(VMEM, VMEM),
@@ -226,8 +227,7 @@
     with jax.named_scope("to_owners"):
         received = exchange(payload, "dp")
     with jax.named_scope("squares"):
-        squares = jnp.sum(received[:, 8:16, :].astype(jnp.float32), axis=0)
-        squares = squares[:, :128] + squares[:, 128:]
+        squares = jnp.sum(received[:, 64:72, :].astype(jnp.float32), axis=0)
         squares = jnp.broadcast_to(squares, (sections // CORES,) + squares.shape)
         squares = exchange(squares, "section", axis_index_groups=along_z)
         squares = lax.all_gather(squares, "section", axis_index_groups=pairs, tiled=True)
@@ -243,23 +243,21 @@
     with jax.named_scope("gather_y"):
         gathered = exchange(copies, "dp", axis_index_groups=along_y)
     with jax.named_scope("gather_x"):
-        copies = pl.pallas_call(
-            copies_kernel,
-            out_shape=jax.ShapeDtypeStruct((XS,) + gathered.shape, jnp.bfloat16),
-            in_specs=[VMEM],
-            out_specs=VMEM,
-            compiler_params=params,
-        )(gathered)
-        gathered = exchange(copies, "dp", axis_index_groups=along_x)
+        pieces = [gathered]
+        for step in range(1, XS):
+            pairs_x = [
+                (x * YS + y, (x + step) % XS * YS + y) for x in range(XS) for y in range(YS)
+            ]
+            pieces.append(lax.ppermute(gathered, "dp", pairs_x))
     with jax.named_scope("join"):
         weights = pl.pallas_call(
             join_kernel,
             out_shape=jax.ShapeDtypeStruct((1, rows, width), jnp.bfloat16),
-            in_specs=[VMEM],
+            in_specs=[SMEM] + [VMEM] * XS,
             out_specs=HBM,
-            scratch_shapes=[pltpu.SemaphoreType.DMA((replicas,))],
-            compiler_params=params,
-        )(gathered.reshape(replicas, rows, narrow))
+            scratch_shapes=[pltpu.SemaphoreType.DMA((XS, YS))],
+            compiler_params=params,
+        )(own_index, *pieces)
     with jax.named_scope("owned"):
         state = jax.ShapeDtypeStruct(olds[0].shape, jnp.float32)
         news = pl.pallas_call(

time: 129 us -> 127 us (0.984)
  starting transfers between devices: 3.67 us -> 7.83 us
  blocking collectives: 102 us -> 98.2 us
  waiting for transfers between devices: 14.5 us -> 12.8 us
    all_to_all x1 -> x0, waiting for transfers between devices: 14.5 us -> none  [local(): gathered = exchange(copies, 'dp', axis_index_groups=along_x)]
    ppermute x0 -> x3, waiting for transfers between devices: none -> 12.8 us  [local(): pieces.append(lax.ppermute(gathered, 'dp', pairs_x))]
    ppermute x0 -> x3, starting transfers between devices: none -> 7.83 us  [local(): pieces.append(lax.ppermute(gathered, 'dp', pairs_x))]
    all_to_all x1, blocking collectives: 21.2 us -> 17.5 us  [local(): received = exchange(payload, 'dp')]
    all_to_all x1 -> x0, starting transfers between devices: 3.67 us -> none  [local(): gathered = exchange(copies, 'dp', axis_index_groups=along_x)]
  transfers between devices with their start and end apart: 1 -> 3, of which waited for: 1 -> 2; matrix products, arithmetic and copies ran while one was open for 0% -> 0% of each run, Pallas kernels for 1% -> 2%
where the time goes in v3:
time: 127 us; the launch traced here: 126 us
  blocking collectives  98.2 us (77%)
  waiting for transfers between devices  12.8 us (10%)
  starting transfers between devices  7.83 us (6%)
  Pallas kernels  4.85 us (4%)
  local copies, waits for them, and re-layouts  1.36 us (1%)
    all_to_all x1, blocking collectives, local(): blocks = exchange(blocks, 'dp', axis_index_groups=along_y)  20.3 us
    all_to_all x1, blocking collectives, local(): blocks = exchange(blocks, 'dp', axis_index_groups=along_x)  17.9 us
    all_to_all x1, blocking collectives, local(): received = exchange(payload, 'dp')  17.5 us
    all_to_all x1, blocking collectives, local(): squares = exchange(squares, 'section', axis_index_groups=along_z)  16.7 us
    all_to_all x1, blocking collectives, local(): gathered = exchange(copies, 'dp', axis_index_groups=along_y)  16.5 us
    ppermute x3, waiting for transfers between devices, local(): pieces.append(lax.ppermute(gathered, 'dp', pairs_x))  12.8 us
    all_gather x1, blocking collectives, local(): lax.all_gather(squares, 'section', axis_index_groups=pairs, tiled=True)  9.29 us
    ppermute x3, starting transfers between devices, local(): pieces.append(lax.ppermute(gathered, 'dp', pairs_x))  7.83 us
  transfers between devices with their start and end apart: 3, of which 2 were waited for; matrix products, arithmetic and copies ran while one was open for 0% of the time, Pallas kernels for 2%

profile of v3, /device:TPU:1, one launch (start us, length us, event | category | flops | bytes accessed | tf_op | source)
XLA Modules:
  0.0 126.1 jit_solution(15897411427345056567)
XLA Ops:
  0.6 0.0 copy-start
  0.6 1.3 %copy-done = bf16[1,1,80,8192]{3,2,1,0:T(8,128)(2,1)S(1)} copy-done((bf16[1,1,80,8192]{3,2,1,0:T(8,128)(2,1)S(1)}, bf16[1,1,80,8192]{3,2,1,0:T(8,128)(2,1)}, u32[]{:S(2)}) %copy-start) | copy-done | bytes 1310744
  1.9 0.1 reduce_x.1
  2.1 17.9 %all_to_all.25 = bf16[4,80,2048]{2,1,0:T(8,128)(2,1)S(1)} all-to-all(bf16[4,80,2048]{2,1,0:T(8,128)(2,1)S(1)} %reduce_x.1), channel_id=1, replica_groups={{0,8,16,24},{1,9,17,25},{2,10,18,26},{3,11,19,27},{4,12,20,28},{5,13,21..., dimensions={0} | all-to-all | bytes 2621440 | tf_op jit(solution)/shard_map/reduce_x/all_to_all | solution.py:211
  20.0 0.0 copy-start.1
  20.0 0.0 copy-start.2
  20.0 0.0 copy-start.3
  20.0 0.0 copy-start.5
  20.0 0.2 reduce_sum.21
  20.3 20.3 %all_to_all.26.parts = bf16[8,80,256]{2,1,0:T(8,128)(2,1)S(1)} all-to-all(bf16[8,80,256]{2,1,0:T(8,128)(2,1)S(1)} %bitcast.27), channel_id=1, replica_groups={{0,1,2,3,4,5,6,7},{8,9,10,11,12,13,14,15},{16,17,18,19,20,21,22,23},{24..., dimensions={0} | all-to-all | bytes 655360 | tf_op jit(solution)/shard_map/reduce_y/all_to_all | solution.py:215
  40.6 0.0 copy-done.1
  40.6 0.0 copy-done.2
  40.6 0.0 copy-done.3
  40.6 0.0 copy-done.5
  40.6 0.7 split.1
  41.2 0.0 copy-start.4
  41.2 17.5 %all_to_all.27.received = bf16[32,72,128]{2,1,0:T(8,128)(2,1)S(1)} all-to-all(bf16[32,72,128]{2,1,0:T(8,128)(2,1)S(1)} %get-tuple-element.11), channel_id=1, replica_groups=mesh['section'=16,'dp'=32] {'dp'}, dimensions={0} | all-to-all | bytes 1179648 | tf_op jit(solution)/shard_map/to_owners/all_to_all | solution.py:228
  58.8 16.7 %all_to_all.28 = f32[8,8,128]{2,1,0:T(8,128)S(1)} all-to-all(f32[8,8,128]{2,1,0:T(8,128)S(1)} %broadcast_in_dim.15), channel_id=1, replica_groups={{0,64,128,192,256,320,384,448},{32,96,160,224,288,352,416,480},{1,65,12..., dimensions={0} | all-to-all | bytes 65536 | tf_op jit(solution)/shard_map/squares/all_to_all | solution.py:232
  75.5 9.3 %all_gather.3.squares = f32[16,8,128]{2,1,0:T(8,128)S(1)} all-gather(f32[8,8,128]{2,1,0:T(8,128)S(1)} %all_to_all.28), channel_id=1, replica_groups={{0,32},{64,96},{128,160},{192,224},{256,288},{320,352},{384,416},{448,4..., dimensions={0}, use_global_device_ids=true | all-gather | bytes 98304 | tf_op jit(solution)/shard_map/squares/all_gather | solution.py:233
  84.8 0.8 columns.1
  85.6 16.5 %all_to_all.29.refs_0_ = bf16[8,80,256]{2,1,0:T(8,128)(2,1)S(1)} all-to-all(bf16[8,80,256]{2,1,0:T(8,128)(2,1)S(1)} %columns.1), channel_id=1, replica_groups={{0,1,2,3,4,5,6,7},{8,9,10,11,12,13,14,15},{16,17,18,19,20,21,22,23},{24..., dimensions={0} | all-to-all | bytes 655360 | tf_op jit(solution)/shard_map/gather_y/all_to_all | solution.py:244
  102.2 2.7 %collective-permute-start.2 = (bf16[8,80,256]{2,1,0:T(8,128)(2,1)S(1)}, bf16[8,80,256]{2,1,0:T(8,128)(2,1)S(1)}, u32[]{:S(2)}, u32[]{:S(2)}) collective-permute-start(bf16[8,80,256]{2,1,0:T(8,128)(2,1)S(1)} %all_to_all.29.refs_0_), channel_id=1, source_target_pairs={{0,24},{1,25},{2,26},{3,27},{4,28},{5,29},{6,30},{7,31},{8,0},{9,1... | collective-permute-start | bytes 983048 | tf_op jit(solution)/shard_map/gather_x/ppermute | solution.py:251
  104.9 3.2 %collective-permute-start.1 = (bf16[8,80,256]{2,1,0:T(8,128)(2,1)S(1)}, bf16[8,80,256]{2,1,0:T(8,128)(2,1)S(1)}, u32[]{:S(2)}, u32[]{:S(2)}) collective-permute-start(bf16[8,80,256]{2,1,0:T(8,128)(2,1)S(1)} %all_to_all.29.refs_0_), channel_id=1, source_target_pairs={{0,16},{1,17},{2,18},{3,19},{4,20},{5,21},{6,22},{7,23},{8,24},{9,... | collective-permute-start | bytes 983048 | tf_op jit(solution)/shard_map/gather_x/ppermute | solution.py:251
  108.1 1.9 %collective-permute-start = (bf16[8,80,256]{2,1,0:T(8,128)(2,1)S(1)}, bf16[8,80,256]{2,1,0:T(8,128)(2,1)S(1)}, u32[]{:S(2)}, u32[]{:S(2)}) collective-permute-start(bf16[8,80,256]{2,1,0:T(8,128)(2,1)S(1)} %all_to_all.29.refs_0_), channel_id=1, source_target_pairs={{0,8},{1,9},{2,10},{3,11},{4,12},{5,13},{6,14},{7,15},{8,16},{9,17... | collective-permute-start | bytes 983048 | tf_op jit(solution)/shard_map/gather_x/ppermute | solution.py:251
  110.0 0.0 copy-done.4
  110.1 1.9 %owned.1 = (f32[8,8192]{1,0:T(8,128)}, f32[8,8192]{1,0:T(8,128)}, f32[8,8192]{1,0:T(8,128)}, f32[8,8192]{1,0:T(8,128)}) custom-call(s32[24]{0:T(128)S(1)} %bitcast.26, s32[1]{0:T(128)} %bitcast.me, f32[16,8,128]{2,1,0:T(8,128)S(1)} %all_gather.3.squares, bf16[32,72,128]{2,1,0:T(8,128)(2,1)S(1)} %all_to_all.27.received, f32[8,8192]{1,0:T(8,128)S(1)} %bitcast.18, ...), custom_call_target="tpu_custom_call" | custom-call | tf_op jit(solution)/shard_map/owned/pallas_call | solution.py:263
  112.0 0.0 collective-permute-done.2.refs_3_
  112.0 3.9 %collective-permute-done.1.refs_2_ = bf16[8,80,256]{2,1,0:T(8,128)(2,1)S(1)} collective-permute-done((bf16[8,80,256]{2,1,0:T(8,128)(2,1)S(1)}, bf16[8,80,256]{2,1,0:T(8,128)(2,1)S(1)}, u32[]{:S(2)}, u32[]{:S(2)}) %collective-permute-start.1) | collective-permute-done | bytes 327712 | tf_op jit(solution)/shard_map/gather_x/ppermute | solution.py:251
  115.9 8.9 %collective-permute-done.refs_1_ = bf16[8,80,256]{2,1,0:T(8,128)(2,1)S(1)} collective-permute-done((bf16[8,80,256]{2,1,0:T(8,128)(2,1)S(1)}, bf16[8,80,256]{2,1,0:T(8,128)(2,1)S(1)}, u32[]{:S(2)}, u32[]{:S(2)}) %collective-permute-start) | collective-permute-done | bytes 327712 | tf_op jit(solution)/shard_map/gather_x/ppermute | solution.py:251
  124.8 1.3 %join.1 = bf16[1,80,8192]{2,1,0:T(8,128)(2,1)} custom-call(s32[1]{0:T(128)} %bitcast.me, bf16[8,80,256]{2,1,0:T(8,128)(2,1)S(1)} %all_to_all.29.refs_0_, bf16[8,80,256]{2,1,0:T(8,128)(2,1)S(1)} %collective-permute-done.refs_1_, bf16[8,80,256]{2,1,0:T(8,128)(2,1)S(1)} %collective-permute-done.1.refs_2_, bf16[8,80,256]{2,1,0:T(8,128)(2,1)S(1)} %collective-permute-done.2.refs_3_), custom_call_target="tpu_custom_call" | custom-call | tf_op jit(solution)/shard_map/join/pallas_call | solution.py:253
  (3 shorter events, 0.1 us)
Async XLA Ops:
  0.6 1.3 %copy-start = (bf16[1,1,80,8192]{3,2,1,0:T(8,128)(2,1)S(1)}, bf16[1,1,80,8192]{3,2,1,0:T(8,128)(2,1)}, u32[]{:S(2)}) copy-start(bf16[1,1,80,8192]{3,2,1,0:T(8,128)(2,1)} %grads.1) | copy-start | bytes 3932164
  20.0 20.6 %copy-start.1 = (f32[1,1,8,8192]{3,2,1,0:T(8,128)S(1)}, f32[1,1,8,8192]{3,2,1,0:T(8,128)}, u32[]{:S(2)}) copy-start(f32[1,1,8,8192]{3,2,1,0:T(8,128)} %param.8) | copy-start | bytes 786436
  20.0 20.6 %copy-start.2 = (f32[1,1,8,8192]{3,2,1,0:T(8,128)S(1)}, f32[1,1,8,8192]{3,2,1,0:T(8,128)}, u32[]{:S(2)}) copy-start(f32[1,1,8,8192]{3,2,1,0:T(8,128)} %param.9) | copy-start | bytes 786436
  20.0 20.6 %copy-start.3 = (f32[1,1,8,8192]{3,2,1,0:T(8,128)S(1)}, f32[1,1,8,8192]{3,2,1,0:T(8,128)}, u32[]{:S(2)}) copy-start(f32[1,1,8,8192]{3,2,1,0:T(8,128)} %param.10) | copy-start | bytes 786436
  20.0 20.6 %copy-start.5 = (s32[1,24]{1,0:T(1,128)S(1)}, s32[1,24]{1,0:T(1,128)}, u32[]{:S(2)}) copy-start(s32[1,24]{1,0:T(1,128)} %param.7) | copy-start | bytes 292
  41.2 68.8 %copy-start.4 = (f32[1,1,8,8192]{3,2,1,0:T(8,128)S(1)}, f32[1,1,8,8192]{3,2,1,0:T(8,128)}, u32[]{:S(2)}) copy-start(f32[1,1,8,8192]{3,2,1,0:T(8,128)} %param.11) | copy-start | bytes 786436
  102.2 9.8 %collective-permute-start.2 = (bf16[8,80,256]{2,1,0:T(8,128)(2,1)S(1)}, bf16[8,80,256]{2,1,0:T(8,128)(2,1)S(1)}, u32[]{:S(2)}, u32[]{:S(2)}) collective-permute-start(bf16[8,80,256]{2,1,0:T(8,128)(2,1)S(1)} %all_to_all.29.refs_0_), channel_id=1, source_target_pairs={{0,24},{1,25},{2,26},{3,27},{4,28},{5,29},{6,30},{7,31},{8,0},{9,1... | collective-permute-start | bytes 983048 | tf_op jit(solution)/shard_map/gather_x/ppermute | solution.py:251
  104.9 10.9 %collective-permute-start.1 = (bf16[8,80,256]{2,1,0:T(8,128)(2,1)S(1)}, bf16[8,80,256]{2,1,0:T(8,128)(2,1)S(1)}, u32[]{:S(2)}, u32[]{:S(2)}) collective-permute-start(bf16[8,80,256]{2,1,0:T(8,128)(2,1)S(1)} %all_to_all.29.refs_0_), channel_id=1, source_target_pairs={{0,16},{1,17},{2,18},{3,19},{4,20},{5,21},{6,22},{7,23},{8,24},{9,... | collective-permute-start | bytes 983048 | tf_op jit(solution)/shard_map/gather_x/ppermute | solution.py:251
  108.1 16.7 %collective-permute-start = (bf16[8,80,256]{2,1,0:T(8,128)(2,1)S(1)}, bf16[8,80,256]{2,1,0:T(8,128)(2,1)S(1)}, u32[]{:S(2)}, u32[]{:S(2)}) collective-permute-start(bf16[8,80,256]{2,1,0:T(8,128)(2,1)S(1)} %all_to_all.29.refs_0_), channel_id=1, source_target_pairs={{0,8},{1,9},{2,10},{3,11},{4,12},{5,13},{6,14},{7,15},{8,16},{9,17... | collective-permute-start | bytes 983048 | tf_op jit(solution)/shard_map/gather_x/ppermute | solution.py:251

commit v4 on v3

--- a/solution.py
+++ b/solution.py
@@ -16,11 +16,6 @@
 decay_rate = 0.1
 average_keep = 0.999
 clip_level = 0.5
-
-XS = 4
-YS = 8
-CORES = 2
-
 
 def tensor_layout(all_rows, slot_rows, layers):
     layer_rows = all_rows // layers
@@ -154,20 +149,14 @@
         move.wait()
 
 
-def join_kernel(me, *refs):
-    blocks, (weights, sems) = refs[:-2], refs[-2:]
-    count, _, width = blocks[0].shape
-    own = lax.div(me[0], count)
-    moves = []
-    for step, block in enumerate(blocks):
-        source = lax.rem(own + (len(blocks) - step), len(blocks))
-        for part in range(count):
-            start = pl.multiple_of((source * count + part) * width, width)
-            moves.append(
-                pltpu.make_async_copy(
-                    block.at[part], weights.at[0, :, pl.ds(start, width)], sems.at[step, part]
-                )
-            )
+def join_kernel(blocks, weights, sems):
+    parts, _, width = blocks.shape
+    moves = [
+        pltpu.make_async_copy(
+            blocks.at[part], weights.at[0, :, pl.ds(part * width, width)], sems.at[part]
+        )
+        for part in range(parts)
+    ]
     for move in moves:
         move.start()
     for move in moves:
@@ -189,30 +178,21 @@
     numel = sections * rows * width
     owner = owners[0]
     own_index = lax.axis_index("dp").astype(jnp.int32).reshape(1)
-    along_x = [[x * YS + y for x in range(XS)] for y in range(YS)]
-    along_y = [[x * YS + y for y in range(YS)] for x in range(XS)]
-    along_z = [list(range(core, sections, CORES)) for core in range(CORES)]
-    pairs = [[z * CORES + core for core in range(CORES)] for z in range(sections // CORES)]
     exchange = functools.partial(lax.all_to_all, split_axis=0, concat_axis=0, tiled=True)
     params = pltpu.CompilerParams(vmem_limit_bytes=LIMIT)
     olds = (master[0, 0], moment[0, 0], second[0, 0], average[0, 0])
     narrow = width // replicas
-    wide = width // XS
-
-    with jax.named_scope("reduce_x"):
+
+    with jax.named_scope("reduce"):
         blocks = pl.pallas_call(
             cut_kernel,
-            out_shape=jax.ShapeDtypeStruct((XS, rows, wide), jnp.bfloat16),
+            out_shape=jax.ShapeDtypeStruct((replicas, rows, narrow), jnp.bfloat16),
             in_specs=[HBM],
             out_specs=VMEM,
-            scratch_shapes=[pltpu.SemaphoreType.DMA((XS,))],
-            compiler_params=pltpu.CompilerParams(vmem_limit_bytes=LIMIT),
+            scratch_shapes=[pltpu.SemaphoreType.DMA((replicas,))],
+            compiler_params=params,
         )(grads)
-        blocks = exchange(blocks, "dp", axis_index_groups=along_x)
-        summed = jnp.sum(blocks.astype(jnp.float32), axis=0).astype(jnp.bfloat16)
-    with jax.named_scope("reduce_y"):
-        blocks = summed.reshape(rows, YS, narrow).transpose(1, 0, 2)
-        blocks = exchange(blocks, "dp", axis_index_groups=along_y)
+        blocks = exchange(blocks, "dp")
     with jax.named_scope("split"):
         mean, payload = pl.pallas_call(
             functools.partial(split_kernel, layout, replicas),
@@ -228,36 +208,27 @@
         received = exchange(payload, "dp")
     with jax.named_scope("squares"):
         squares = jnp.sum(received[:, 64:72, :].astype(jnp.float32), axis=0)
-        squares = jnp.broadcast_to(squares, (sections // CORES,) + squares.shape)
-        squares = exchange(squares, "section", axis_index_groups=along_z)
-        squares = lax.all_gather(squares, "section", axis_index_groups=pairs, tiled=True)
+        squares = jnp.broadcast_to(squares, (sections,) + squares.shape)
+        squares = exchange(squares, "section")
     with jax.named_scope("columns"):
         copies = pl.pallas_call(
             functools.partial(column_kernel, layout, numel),
-            out_shape=jax.ShapeDtypeStruct((YS, rows, narrow), jnp.bfloat16),
+            out_shape=jax.ShapeDtypeStruct((replicas, rows, narrow), jnp.bfloat16),
             in_specs=[SMEM, VMEM, VMEM, VMEM],
             out_specs=VMEM,
             scratch_shapes=[pltpu.VMEM((rows, narrow), jnp.float32)] * 4,
             compiler_params=params,
         )(owner, squares, mean, received)
-    with jax.named_scope("gather_y"):
-        gathered = exchange(copies, "dp", axis_index_groups=along_y)
-    with jax.named_scope("gather_x"):
-        pieces = [gathered]
-        for step in range(1, XS):
-            pairs_x = [
-                (x * YS + y, (x + step) % XS * YS + y) for x in range(XS) for y in range(YS)
-            ]
-            pieces.append(lax.ppermute(gathered, "dp", pairs_x))
-    with jax.named_scope("join"):
+    with jax.named_scope("gather"):
+        gathered = exchange(copies, "dp")
         weights = pl.pallas_call(
             join_kernel,
             out_shape=jax.ShapeDtypeStruct((1, rows, width), jnp.bfloat16),
-            in_specs=[SMEM] + [VMEM] * XS,
+            in_specs=[VMEM],
             out_specs=HBM,
-            scratch_shapes=[pltpu.SemaphoreType.DMA((XS, YS))],
-            compiler_params=params,
-        )(own_index, *pieces)
+            scratch_shapes=[pltpu.SemaphoreType.DMA((replicas,))],
+            compiler_params=params,
+        )(gathered)
     with jax.named_scope("owned"):
         state = jax.ShapeDtypeStruct(olds[0].shape, jnp.float32)
         news = pl.pallas_call(

time: 127 us -> 132 us (1.039)
  waiting for transfers between devices: 12.8 us -> 29.9 us
  blocking collectives: 98.2 us -> 87 us
  starting transfers between devices: 7.83 us -> 5.01 us
  Pallas kernels: 4.85 us -> 6.55 us
    all_to_all x0 -> x1, waiting for transfers between devices: none -> 29.9 us  [local(): gathered = exchange(copies, 'dp')]
    ppermute x3 -> x0, waiting for transfers between devices: 12.8 us -> none  [local(): pieces.append(lax.ppermute(gathered, 'dp', pairs_x))]
    all_gather x1 -> x0, blocking collectives: 9.29 us -> none  [local(): lax.all_gather(squares, 'section', axis_index_groups=pairs, tiled=True)]
    ppermute x3 -> x0, starting transfers between devices: 7.83 us -> none  [local(): pieces.append(lax.ppermute(gathered, 'dp', pairs_x))]
    all_to_all x4 -> x2, blocking collectives: 71.4 us -> 64.9 us  [the longest x1 42.9 us: local(): blocks = exchange(blocks, 'dp')]
    all_to_all x0 -> x1, starting transfers between devices: none -> 5.01 us  [local(): gathered = exchange(copies, 'dp')]
    all_to_all x1, blocking collectives: 17.5 us -> 22.1 us  [local(): received = exchange(payload, 'dp')]
  transfers between devices with their start and end apart: 3 -> 1, of which waited for: 2 -> 1; matrix products, arithmetic and copies ran while one was open for 0% -> 0% of each run, Pallas kernels for 2% -> 1%
where the time goes in v4:
time: 132 us; the launch traced here: 130 us
  blocking collectives  87 us (66%)
  waiting for transfers between devices  29.9 us (23%)
  Pallas kernels  6.55 us (5%)
  starting transfers between devices  5.01 us (4%)
  local copies, waits for them, and re-layouts  1.35 us (1%)
    all_to_all x1, blocking collectives, local(): blocks = exchange(blocks, 'dp')  42.9 us
    all_to_all x1, waiting for transfers between devices, local(): gathered = exchange(copies, 'dp')  29.9 us
    all_to_all x1, blocking collectives, local(): received = exchange(payload, 'dp')  22.1 us
    all_to_all x1, blocking collectives, local(): squares = exchange(squares, 'section')  22 us
    all_to_all x1, starting transfers between devices, local(): gathered = exchange(copies, 'dp')  5.01 us
  transfers between devices with their start and end apart: 1, of which 1 were waited for; matrix products, arithmetic and copies ran while one was open for 0% of the time, Pallas kernels for 1%

profile of v4, /device:TPU:1, one launch (start us, length us, event | category | flops | bytes accessed | tf_op | source)
XLA Modules:
  0.0 130.5 jit_solution(5938244269677284306)
XLA Ops:
  0.6 0.0 copy-start
  0.6 1.3 %copy-done = bf16[1,1,80,8192]{3,2,1,0:T(8,128)(2,1)S(1)} copy-done((bf16[1,1,80,8192]{3,2,1,0:T(8,128)(2,1)S(1)}, bf16[1,1,80,8192]{3,2,1,0:T(8,128)(2,1)}, u32[]{:S(2)}) %copy-start) | copy-done | bytes 1310744
  1.9 0.6 reduce.1
  2.5 0.0 copy-start.1
  2.5 0.0 copy-start.2
  2.5 0.0 copy-start.3
  2.6 0.0 copy-start.5
  2.6 42.9 %all_to_all.20.parts = bf16[32,80,256]{2,1,0:T(8,128)(2,1)S(1)} all-to-all(bf16[32,80,256]{2,1,0:T(8,128)(2,1)S(1)} %reduce.1), channel_id=1, replica_groups=mesh['section'=16,'dp'=32] {'dp'}, dimensions={0} | all-to-all | bytes 2621440 | tf_op jit(solution)/shard_map/reduce/all_to_all | solution.py:195
  45.5 0.0 copy-done.1
  45.5 0.0 copy-done.2
  45.5 0.0 copy-done.3
  45.5 0.0 copy-done.5
  45.5 0.8 split.1
  46.3 22.1 %all_to_all.21.received = bf16[32,72,128]{2,1,0:T(8,128)(2,1)S(1)} all-to-all(bf16[32,72,128]{2,1,0:T(8,128)(2,1)S(1)} %get-tuple-element.11), channel_id=1, replica_groups=mesh['section'=16,'dp'=32] {'dp'}, dimensions={0} | all-to-all | bytes 1179648 | tf_op jit(solution)/shard_map/to_owners/all_to_all | solution.py:208
  68.4 22.0 %all_to_all.22.squares = f32[16,8,128]{2,1,0:T(8,128)S(1)} all-to-all(f32[16,8,128]{2,1,0:T(8,128)S(1)} %broadcast_in_dim.15), channel_id=1, replica_groups=mesh['section'=16,'dp'=32] {'section'}, dimensions={0} | all-to-all | bytes 131072 | tf_op jit(solution)/shard_map/squares/all_to_all | solution.py:212
  90.4 2.0 %columns.1 = bf16[32,80,256]{2,1,0:T(8,128)(2,1)} custom-call(s32[24]{0:T(128)S(1)} %bitcast.18, f32[16,8,128]{2,1,0:T(8,128)S(1)} %all_to_all.22.squares, f32[80,256]{1,0:T(8,128)S(1)} %get-tuple-element.12.mean, bf16[32,72,128]{2,1,0:T(8,128)(2,1)S(1)} %all_to_all.21.received), custom_call_target="tpu_custom_call" | custom-call | tf_op jit(solution)/shard_map/columns/pallas_call | solution.py:214
  92.4 0.0 copy-start.4
  92.4 5.0 %all-to-all-start.3 = ((bf16[32,80,256]{2,1,0:T(8,128)(2,1)}), bf16[32,80,256]{2,1,0:T(8,128)(2,1)S(1)}, u32[]{:S(2)}, u32[]{:S(2)}) async-start(bf16[32,80,256]{2,1,0:T(8,128)(2,1)} %columns.1), calls=%async_computation.3 | async-start | bytes 2621440 | tf_op jit(solution)/shard_map/gather/all_to_all | solution.py:223
  97.4 0.0 copy-done.4
  97.4 1.9 %owned.1 = (f32[8,8192]{1,0:T(8,128)}, f32[8,8192]{1,0:T(8,128)}, f32[8,8192]{1,0:T(8,128)}, f32[8,8192]{1,0:T(8,128)}) custom-call(s32[24]{0:T(128)S(1)} %bitcast.19, s32[1]{0:T(128)} %bitcast.4.me, f32[16,8,128]{2,1,0:T(8,128)S(1)} %all_to_all.22.squares, bf16[32,72,128]{2,1,0:T(8,128)(2,1)S(1)} %all_to_all.21.received, f32[8,8192]{1,0:T(8,128)S(1)} %bitcast.11, ...), custom_call_target="tpu_custom_call" | custom-call | tf_op jit(solution)/shard_map/owned/pallas_call | solution.py:234
  99.3 29.9 %all-to-all-done.3.blocks = bf16[32,80,256]{2,1,0:T(8,128)(2,1)S(1)} async-done(((bf16[32,80,256]{2,1,0:T(8,128)(2,1)}), bf16[32,80,256]{2,1,0:T(8,128)(2,1)S(1)}, u32[]{:S(2)}, u32[]{:S(2)}) %all-to-all-start.3) | async-done | bytes 1310752 | tf_op jit(solution)/shard_map/gather/all_to_all | solution.py:223
  129.2 1.3 %gather.1 = bf16[1,80,8192]{2,1,0:T(8,128)(2,1)} custom-call(bf16[32,80,256]{2,1,0:T(8,128)(2,1)S(1)} %all-to-all-done.3.blocks), custom_call_target="tpu_custom_call" | custom-call | tf_op jit(solution)/shard_map/gather/pallas_call | solution.py:224
  (2 shorter events, 0.0 us)
Async XLA Ops:
  0.6 1.3 %copy-start = (bf16[1,1,80,8192]{3,2,1,0:T(8,128)(2,1)S(1)}, bf16[1,1,80,8192]{3,2,1,0:T(8,128)(2,1)}, u32[]{:S(2)}) copy-start(bf16[1,1,80,8192]{3,2,1,0:T(8,128)(2,1)} %grads.1) | copy-start | bytes 3932164
  2.5 42.9 %copy-start.1 = (f32[1,1,8,8192]{3,2,1,0:T(8,128)S(1)}, f32[1,1,8,8192]{3,2,1,0:T(8,128)}, u32[]{:S(2)}) copy-start(f32[1,1,8,8192]{3,2,1,0:T(8,128)} %param.8) | copy-start | bytes 786436
  2.5 42.9 %copy-start.2 = (f32[1,1,8,8192]{3,2,1,0:T(8,128)S(1)}, f32[1,1,8,8192]{3,2,1,0:T(8,128)}, u32[]{:S(2)}) copy-start(f32[1,1,8,8192]{3,2,1,0:T(8,128)} %param.9) | copy-start | bytes 786436
  2.5 42.9 %copy-start.3 = (f32[1,1,8,8192]{3,2,1,0:T(8,128)S(1)}, f32[1,1,8,8192]{3,2,1,0:T(8,128)}, u32[]{:S(2)}) copy-start(f32[1,1,8,8192]{3,2,1,0:T(8,128)} %param.10) | copy-start | bytes 786436
  2.6 42.9 %copy-start.5 = (s32[1,24]{1,0:T(1,128)S(1)}, s32[1,24]{1,0:T(1,128)}, u32[]{:S(2)}) copy-start(s32[1,24]{1,0:T(1,128)} %param.7) | copy-start | bytes 292
  92.4 5.0 %copy-start.4 = (f32[1,1,8,8192]{3,2,1,0:T(8,128)S(1)}, f32[1,1,8,8192]{3,2,1,0:T(8,128)}, u32[]{:S(2)}) copy-start(f32[1,1,8,8192]{3,2,1,0:T(8,128)} %param.11) | copy-start | bytes 786436
  92.4 36.8 %all-to-all-start.3 = ((bf16[32,80,256]{2,1,0:T(8,128)(2,1)}), bf16[32,80,256]{2,1,0:T(8,128)(2,1)S(1)}, u32[]{:S(2)}, u32[]{:S(2)}) async-start(bf16[32,80,256]{2,1,0:T(8,128)(2,1)} %columns.1), calls=%async_computation.3 | async-start | bytes 2621440 | tf_op jit(solution)/shard_map/gather/all_to_all | solution.py:223

commit v5 on v3

--- a/solution.py
+++ b/solution.py
@@ -19,7 +19,6 @@
 
 XS = 4
 YS = 8
-CORES = 2
 
 
 def tensor_layout(all_rows, slot_rows, layers):
@@ -113,31 +112,59 @@
         copies[copy] = weights
 
 
-def owner_kernel(
-    layout, numel, owner, me, squares, received, master, moment, second, average,
-    master_out, moment_out, second_out, average_out,
+def finish_kernel(
+    layout, numel, owner, squares, received, master, moment, second, average, blocks,
+    weights, master_out, moment_out, second_out, average_out,
+    master_new, moment_new, second_new, average_new, weight_sems, state_sems,
 ):
+    parts, _, width = blocks.shape
+    moves = []
+    for part in range(parts):
+        moves.append(
+            pltpu.make_async_copy(
+                blocks.at[part], weights.at[0, :, pl.ds(part * width, width)], weight_sems.at[part]
+            )
+        )
+        moves[-1].start()
     factor = clip_factor(jnp.sum(squares[...]), numel)
+    me = lax.axis_index("dp")
     count = jnp.int32(0)
     flag = jnp.float32(0.0)
     for tensor, (start, rows, decay) in enumerate(layout):
-        mine = owner[tensor] == me[0]
+        mine = owner[tensor] == me
         count = jnp.where(mine, rows, count)
         flag = jnp.where(mine, decay, flag)
-    width = 2 * received.shape[2]
     used = lax.broadcasted_iota(jnp.int32, (8, width), 0) < count
-    for source in range(received.shape[0]):
-        columns = slice(source * width, (source + 1) * width)
-        grad = received[source, 0:16, :].astype(jnp.float32)
-        grad = jnp.concatenate([grad[0:8], grad[8:16]], axis=1)
-        olds = (master[:, columns], moment[:, columns], second[:, columns], average[:, columns])
-        moment_new, second_new = adamw_moments(grad, olds[1], olds[2], factor)
-        master_new = adamw_master(olds[0], moment_new, second_new, flag)
-        average_new = average_keep * olds[3] + (1.0 - average_keep) * master_new
-        master_out[:, columns] = jnp.where(used, master_new, olds[0])
-        moment_out[:, columns] = jnp.where(used, moment_new, olds[1])
-        second_out[:, columns] = jnp.where(used, second_new, olds[2])
-        average_out[:, columns] = jnp.where(used, average_new, olds[3])
+    pairs = (
+        (master_new, master_out), (moment_new, moment_out),
+        (second_new, second_out), (average_new, average_out),
+    )
+    pieces = 4
+    stretch = parts * width // pieces
+    for piece in range(pieces):
+        for source in range(piece * parts // pieces, (piece + 1) * parts // pieces):
+            columns = slice(source * width, (source + 1) * width)
+            grad = received[source, 0:16, :].astype(jnp.float32)
+            grad = jnp.concatenate([grad[0:8], grad[8:16]], axis=1)
+            olds = (
+                master[0, 0, :, columns], moment[0, 0, :, columns],
+                second[0, 0, :, columns], average[0, 0, :, columns],
+            )
+            first, squared = adamw_moments(grad, olds[1], olds[2], factor)
+            whole = adamw_master(olds[0], first, squared, flag)
+            mixed = average_keep * olds[3] + (1.0 - average_keep) * whole
+            for (target, _), new, old in zip(pairs, (whole, first, squared, mixed), olds):
+                target[:, columns] = jnp.where(used, new, old)
+        for place, (source, target) in enumerate(pairs):
+            columns = pl.ds(piece * stretch, stretch)
+            moves.append(
+                pltpu.make_async_copy(
+                    source.at[:, columns], target.at[0, 0, :, columns], state_sems.at[place, piece]
+                )
+            )
+            moves[-1].start()
+    for move in moves:
+        move.wait()
 
 
 def cut_kernel(grads, blocks, sems):
@@ -154,24 +181,9 @@
         move.wait()
 
 
-def join_kernel(me, *refs):
-    blocks, (weights, sems) = refs[:-2], refs[-2:]
-    count, _, width = blocks[0].shape
-    own = lax.div(me[0], count)
-    moves = []
-    for step, block in enumerate(blocks):
-        source = lax.rem(own + (len(blocks) - step), len(blocks))
-        for part in range(count):
-            start = pl.multiple_of((source * count + part) * width, width)
-            moves.append(
-                pltpu.make_async_copy(
-                    block.at[part], weights.at[0, :, pl.ds(start, width)], sems.at[step, part]
-                )
-            )
-    for move in moves:
-        move.start()
-    for move in moves:
-        move.wait()
+def copies_kernel(block, copies):
+    for copy in range(copies.shape[0]):
+        copies[copy] = block[...]
 
 
 VMEM = pl.BlockSpec(memory_space=pltpu.VMEM)
@@ -188,11 +200,8 @@
     sections = lax.axis_size("section")
     numel = sections * rows * width
     owner = owners[0]
-    own_index = lax.axis_index("dp").astype(jnp.int32).reshape(1)
     along_x = [[x * YS + y for x in range(XS)] for y in range(YS)]
     along_y = [[x * YS + y for y in range(YS)] for x in range(XS)]
-    along_z = [list(range(core, sections, CORES)) for core in range(CORES)]
-    pairs = [[z * CORES + core for core in range(CORES)] for z in range(sections // CORES)]
     exchange = functools.partial(lax.all_to_all, split_axis=0, concat_axis=0, tiled=True)
     params = pltpu.CompilerParams(vmem_limit_bytes=LIMIT)
     olds = (master[0, 0], moment[0, 0], second[0, 0], average[0, 0])
@@ -228,9 +237,8 @@
         received = exchange(payload, "dp")
     with jax.named_scope("squares"):
         squares = jnp.sum(received[:, 64:72, :].astype(jnp.float32), axis=0)
-        squares = jnp.broadcast_to(squares, (sections // CORES,) + squares.shape)
-        squares = exchange(squares, "section", axis_index_groups=along_z)
-        squares = lax.all_gather(squares, "section", axis_index_groups=pairs, tiled=True)
+        squares = jnp.broadcast_to(squares, (sections,) + squares.shape)
+        squares = exchange(squares, "section")
     with jax.named_scope("columns"):
         copies = pl.pallas_call(
             functools.partial(column_kernel, layout, numel),
@@ -243,31 +251,29 @@
     with jax.named_scope("gather_y"):
         gathered = exchange(copies, "dp", axis_index_groups=along_y)
     with jax.named_scope("gather_x"):
-        pieces = [gathered]
-        for step in range(1, XS):
-            pairs_x = [
-                (x * YS + y, (x + step) % XS * YS + y) for x in range(XS) for y in range(YS)
-            ]
-            pieces.append(lax.ppermute(gathered, "dp", pairs_x))
-    with jax.named_scope("join"):
-        weights = pl.pallas_call(
-            join_kernel,
-            out_shape=jax.ShapeDtypeStruct((1, rows, width), jnp.bfloat16),
-            in_specs=[SMEM] + [VMEM] * XS,
-            out_specs=HBM,
-            scratch_shapes=[pltpu.SemaphoreType.DMA((XS, YS))],
-            compiler_params=params,
-        )(own_index, *pieces)
-    with jax.named_scope("owned"):
-        state = jax.ShapeDtypeStruct(olds[0].shape, jnp.float32)
-        news = pl.pallas_call(
-            functools.partial(owner_kernel, layout, numel),
-            out_shape=(state,) * 4,
-            in_specs=[SMEM, SMEM] + [VMEM] * 6,
-            out_specs=(VMEM,) * 4,
-            compiler_params=params,
-        )(owner, own_index, squares, received, *olds)
-    return (weights,) + tuple(new[None, None] for new in news)
+        copies = pl.pallas_call(
+            copies_kernel,
+            out_shape=jax.ShapeDtypeStruct((XS,) + gathered.shape, jnp.bfloat16),
+            in_specs=[VMEM],
+            out_specs=VMEM,
+            compiler_params=params,
+        )(gathered)
+        gathered = exchange(copies, "dp", axis_index_groups=along_x)
+    with jax.named_scope("finish"):
+        outs = pl.pallas_call(
+            functools.partial(finish_kernel, layout, numel),
+            out_shape=(jax.ShapeDtypeStruct((1, rows, width), jnp.bfloat16),)
+            + (jax.ShapeDtypeStruct(master.shape, jnp.float32),) * 4,
+            in_specs=[SMEM] + [VMEM] * 7,
+            out_specs=(HBM,) * 5,
+            scratch_shapes=[pltpu.VMEM(master.shape[2:], jnp.float32)] * 4
+            + [pltpu.SemaphoreType.DMA((replicas,)), pltpu.SemaphoreType.DMA((4, 4))],
+            compiler_params=params,
+        )(
+            owner, squares, received, master, moment, second, average,
+            gathered.reshape(replicas, rows, narrow),
+        )
+    return tuple(outs)
 
 
 def solution(mesh):

time: 127 us -> 123 us (0.969)
  blocking collectives: 98.2 us -> 116 us
  waiting for transfers between devices: 12.8 us -> 0 us
  starting transfers between devices: 7.83 us -> 0 us
    all_to_all x1 -> x2, blocking collectives: 16.7 us -> 43.6 us  [the longest x1 24.3 us: local(): squares = exchange(squares, 'section')]
    ppermute x3 -> x0, waiting for transfers between devices: 12.8 us -> none  [local(): pieces.append(lax.ppermute(gathered, 'dp', pairs_x))]
    all_gather x1 -> x0, blocking collectives: 9.29 us -> none  [local(): lax.all_gather(squares, 'section', axis_index_groups=pairs, tiled=True)]
    ppermute x3 -> x0, starting transfers between devices: 7.83 us -> none  [local(): pieces.append(lax.ppermute(gathered, 'dp', pairs_x))]
  transfers between devices with their start and end apart: 3 -> 0, of which waited for: 2 -> 0; matrix products, arithmetic and copies ran while one was open for 0% -> 0% of each run, Pallas kernels for 2% -> 0%
where the time goes in v5:
time: 123 us
  blocking collectives  116 us (94%)
  Pallas kernels  4.18 us (3%)
  local copies, waits for them, and re-layouts  1.36 us (1%)
    all_to_all x1, blocking collectives, local(): squares = exchange(squares, 'section')  24.3 us
    all_to_all x1, blocking collectives, local(): blocks = exchange(blocks, 'dp', axis_index_groups=along_y)  20.3 us
    all_to_all x1, blocking collectives, local(): gathered = exchange(copies, 'dp', axis_index_groups=along_x)  19.3 us
    all_to_all x1, blocking collectives, local(): blocks = exchange(blocks, 'dp', axis_index_groups=along_x)  17.9 us
    all_to_all x1, blocking collectives, local(): received = exchange(payload, 'dp')  17.4 us
    all_to_all x1, blocking collectives, local(): gathered = exchange(copies, 'dp', axis_index_groups=along_y)  16.9 us
    pallas_call x1, Pallas kernels, local(): pl.pallas_call(functools.partial(finish_kernel, layout, numel), out_shape...  2.47 us

profile of v5, /device:TPU:1, one launch (start us, length us, event | category | flops | bytes accessed | tf_op | source)
XLA Modules:
  0.0 122.5 jit_solution(8519684581760637306)
XLA Ops:
  0.6 0.0 copy-start
  0.6 1.3 %copy-done = bf16[1,1,80,8192]{3,2,1,0:T(8,128)(2,1)S(1)} copy-done((bf16[1,1,80,8192]{3,2,1,0:T(8,128)(2,1)S(1)}, bf16[1,1,80,8192]{3,2,1,0:T(8,128)(2,1)}, u32[]{:S(2)}) %copy-start) | copy-done | bytes 1310744
  1.9 0.1 reduce_x.1
  2.1 17.9 %all_to_all.30 = bf16[4,80,2048]{2,1,0:T(8,128)(2,1)S(1)} all-to-all(bf16[4,80,2048]{2,1,0:T(8,128)(2,1)S(1)} %reduce_x.1), channel_id=1, replica_groups={{0,8,16,24},{1,9,17,25},{2,10,18,26},{3,11,19,27},{4,12,20,28},{5,13,21..., dimensions={0} | all-to-all | bytes 2621440 | tf_op jit(solution)/shard_map/reduce_x/all_to_all | solution.py:220
  20.0 0.0 copy-start.1
  20.0 0.0 copy-start.2
  20.0 0.0 copy-start.3
  20.0 0.0 copy-start.5
  20.0 0.2 reduce_sum.21
  20.3 20.3 %all_to_all.31.parts = bf16[8,80,256]{2,1,0:T(8,128)(2,1)S(1)} all-to-all(bf16[8,80,256]{2,1,0:T(8,128)(2,1)S(1)} %bitcast.19), channel_id=1, replica_groups={{0,1,2,3,4,5,6,7},{8,9,10,11,12,13,14,15},{16,17,18,19,20,21,22,23},{24..., dimensions={0} | all-to-all | bytes 655360 | tf_op jit(solution)/shard_map/reduce_y/all_to_all | solution.py:224
  40.6 0.0 copy-done.1
  40.6 0.0 copy-done.2
  40.6 0.0 copy-done.3
  40.6 0.0 copy-done.5
  40.6 0.7 split.1
  41.2 17.4 %all_to_all.32.received = bf16[32,72,128]{2,1,0:T(8,128)(2,1)S(1)} all-to-all(bf16[32,72,128]{2,1,0:T(8,128)(2,1)S(1)} %get-tuple-element.7), channel_id=1, replica_groups=mesh['section'=16,'dp'=32] {'dp'}, dimensions={0} | all-to-all | bytes 1179648 | tf_op jit(solution)/shard_map/to_owners/all_to_all | solution.py:237
  58.6 24.3 %all_to_all.33.squares = f32[16,8,128]{2,1,0:T(8,128)S(1)} all-to-all(f32[16,8,128]{2,1,0:T(8,128)S(1)} %broadcast_in_dim.3), channel_id=1, replica_groups=mesh['section'=16,'dp'=32] {'section'}, dimensions={0} | all-to-all | bytes 131072 | tf_op jit(solution)/shard_map/squares/all_to_all | solution.py:241
  82.9 0.8 columns.1
  83.8 16.9 %all_to_all.34.block = bf16[8,80,256]{2,1,0:T(8,128)(2,1)S(1)} all-to-all(bf16[8,80,256]{2,1,0:T(8,128)(2,1)S(1)} %columns.1), channel_id=1, replica_groups={{0,1,2,3,4,5,6,7},{8,9,10,11,12,13,14,15},{16,17,18,19,20,21,22,23},{24..., dimensions={0} | all-to-all | bytes 655360 | tf_op jit(solution)/shard_map/gather_y/all_to_all | solution.py:252
  100.6 0.1 gather_x.1
  100.7 0.0 copy-start.4
  100.7 19.3 %all_to_all.35 = bf16[4,8,80,256]{3,2,1,0:T(8,128)(2,1)S(1)} all-to-all(bf16[4,8,80,256]{3,2,1,0:T(8,128)(2,1)S(1)} %gather_x.1), channel_id=1, replica_groups={{0,8,16,24},{1,9,17,25},{2,10,18,26},{3,11,19,27},{4,12,20,28},{5,13,21..., dimensions={0} | all-to-all | bytes 2621440 | tf_op jit(solution)/shard_map/gather_x/all_to_all | solution.py:261
  120.1 0.0 copy-done.4
  120.1 2.5 %finish.1 = (bf16[1,80,8192]{2,1,0:T(8,128)(2,1)}, f32[1,1,8,8192]{3,2,1,0:T(8,128)}, f32[1,1,8,8192]{3,2,1,0:T(8,128)}, f32[1,1,8,8192]{3,2,1,0:T(8,128)}, f32[1,1,8,8192]{3,2,1,0:T(8,128)}) custom-call(s32[24]{0:T(128)S(1)} %bitcast.18, f32[16,8,128]{2,1,0:T(8,128)S(1)} %all_to_all.33.squares, bf16[32,72,128]{2,1,0:T(8,128)(2,1)S(1)} %all_to_all.32.received, ...), custom_call_target="tpu_custom_call" | custom-call | tf_op jit(solution)/shard_map/finish/pallas_call | solution.py:263
  (3 shorter events, 0.1 us)
Async XLA Ops:
  0.6 1.3 %copy-start = (bf16[1,1,80,8192]{3,2,1,0:T(8,128)(2,1)S(1)}, bf16[1,1,80,8192]{3,2,1,0:T(8,128)(2,1)}, u32[]{:S(2)}) copy-start(bf16[1,1,80,8192]{3,2,1,0:T(8,128)(2,1)} %grads.1) | copy-start | bytes 3932164
  20.0 20.6 %copy-start.1 = (f32[1,1,8,8192]{3,2,1,0:T(8,128)S(1)}, f32[1,1,8,8192]{3,2,1,0:T(8,128)}, u32[]{:S(2)}) copy-start(f32[1,1,8,8192]{3,2,1,0:T(8,128)} %master.1) | copy-start | bytes 786436
  20.0 20.6 %copy-start.2 = (f32[1,1,8,8192]{3,2,1,0:T(8,128)S(1)}, f32[1,1,8,8192]{3,2,1,0:T(8,128)}, u32[]{:S(2)}) copy-start(f32[1,1,8,8192]{3,2,1,0:T(8,128)} %moment.1) | copy-start | bytes 786436
  20.0 20.6 %copy-start.3 = (f32[1,1,8,8192]{3,2,1,0:T(8,128)S(1)}, f32[1,1,8,8192]{3,2,1,0:T(8,128)}, u32[]{:S(2)}) copy-start(f32[1,1,8,8192]{3,2,1,0:T(8,128)} %second.1) | copy-start | bytes 786436
  20.0 20.6 %copy-start.5 = (s32[1,24]{1,0:T(1,128)S(1)}, s32[1,24]{1,0:T(1,128)}, u32[]{:S(2)}) copy-start(s32[1,24]{1,0:T(1,128)} %param.7) | copy-start | bytes 292
  100.7 19.3 %copy-start.4 = (f32[1,1,8,8192]{3,2,1,0:T(8,128)S(1)}, f32[1,1,8,8192]{3,2,1,0:T(8,128)}, u32[]{:S(2)}) copy-start(f32[1,1,8,8192]{3,2,1,0:T(8,128)} %average.1) | copy-start | bytes 786436

commit v6 on v4

--- a/solution.py
+++ b/solution.py
@@ -16,6 +16,10 @@
 decay_rate = 0.1
 average_keep = 0.999
 clip_level = 0.5
+
+XS = 4
+YS = 8
+
 
 def tensor_layout(all_rows, slot_rows, layers):
     layer_rows = all_rows // layers
@@ -38,10 +42,8 @@
 
 
 def adamw_master(master, moment_new, second_new, decay):
-    direction = (
-        moment_new
-        / (1.0 - beta_one**STEP)
-        / (jnp.sqrt(second_new / (1.0 - beta_two**STEP)) + epsilon)
+    direction = (moment_new * (1.0 / (1.0 - beta_one**STEP))) / (
+        jnp.sqrt(second_new * (1.0 / (1.0 - beta_two**STEP))) + epsilon
     )
     return master - learn_rate * (direction + decay_rate * decay * master)
 
@@ -109,14 +111,15 @@
 
 
 def owner_kernel(
-    layout, numel, owner, me, squares, received, master, moment, second, average,
-    master_out, moment_out, second_out, average_out,
+    layout, numel, owner, squares, received, master, moment, second, average,
+    master_out, moment_out, second_out, average_out, done,
 ):
     factor = clip_factor(jnp.sum(squares[...]), numel)
+    me = lax.axis_index("dp")
     count = jnp.int32(0)
     flag = jnp.float32(0.0)
     for tensor, (start, rows, decay) in enumerate(layout):
-        mine = owner[tensor] == me[0]
+        mine = owner[tensor] == me
         count = jnp.where(mine, rows, count)
         flag = jnp.where(mine, decay, flag)
     width = 2 * received.shape[2]
@@ -133,6 +136,7 @@
         moment_out[:, columns] = jnp.where(used, moment_new, olds[1])
         second_out[:, columns] = jnp.where(used, second_new, olds[2])
         average_out[:, columns] = jnp.where(used, average_new, olds[3])
+    done[...] = jnp.zeros_like(done)
 
 
 def cut_kernel(grads, blocks, sems):
@@ -149,6 +153,11 @@
         move.wait()
 
 
+def copies_kernel(block, after, copies):
+    for copy in range(copies.shape[0]):
+        copies[copy] = block[...]
+
+
 def join_kernel(blocks, weights, sems):
     parts, _, width = blocks.shape
     moves = [
@@ -177,22 +186,28 @@
     sections = lax.axis_size("section")
     numel = sections * rows * width
     owner = owners[0]
-    own_index = lax.axis_index("dp").astype(jnp.int32).reshape(1)
+    along_x = [[x * YS + y for x in range(XS)] for y in range(YS)]
+    along_y = [[x * YS + y for y in range(YS)] for x in range(XS)]
     exchange = functools.partial(lax.all_to_all, split_axis=0, concat_axis=0, tiled=True)
     params = pltpu.CompilerParams(vmem_limit_bytes=LIMIT)
     olds = (master[0, 0], moment[0, 0], second[0, 0], average[0, 0])
     narrow = width // replicas
-
-    with jax.named_scope("reduce"):
+    wide = width // XS
+
+    with jax.named_scope("reduce_x"):
         blocks = pl.pallas_call(
             cut_kernel,
-            out_shape=jax.ShapeDtypeStruct((replicas, rows, narrow), jnp.bfloat16),
+            out_shape=jax.ShapeDtypeStruct((XS, rows, wide), jnp.bfloat16),
             in_specs=[HBM],
             out_specs=VMEM,
-            scratch_shapes=[pltpu.SemaphoreType.DMA((replicas,))],
-            compiler_params=params,
+            scratch_shapes=[pltpu.SemaphoreType.DMA((XS,))],
+            compiler_params=pltpu.CompilerParams(vmem_limit_bytes=LIMIT),
         )(grads)
-        blocks = exchange(blocks, "dp")
+        blocks = exchange(blocks, "dp", axis_index_groups=along_x)
+        summed = jnp.sum(blocks.astype(jnp.float32), axis=0).astype(jnp.bfloat16)
+    with jax.named_scope("reduce_y"):
+        blocks = summed.reshape(rows, YS, narrow).transpose(1, 0, 2)
+        blocks = exchange(blocks, "dp", axis_index_groups=along_y)
     with jax.named_scope("split"):
         mean, payload = pl.pallas_call(
             functools.partial(split_kernel, layout, replicas),
@@ -213,14 +228,33 @@
     with jax.named_scope("columns"):
         copies = pl.pallas_call(
             functools.partial(column_kernel, layout, numel),
-            out_shape=jax.ShapeDtypeStruct((replicas, rows, narrow), jnp.bfloat16),
+            out_shape=jax.ShapeDtypeStruct((YS, rows, narrow), jnp.bfloat16),
             in_specs=[SMEM, VMEM, VMEM, VMEM],
             out_specs=VMEM,
             scratch_shapes=[pltpu.VMEM((rows, narrow), jnp.float32)] * 4,
             compiler_params=params,
         )(owner, squares, mean, received)
-    with jax.named_scope("gather"):
-        gathered = exchange(copies, "dp")
+    with jax.named_scope("gather_y"):
+        gathered = exchange(copies, "dp", axis_index_groups=along_y)
+    with jax.named_scope("owned"):
+        state = jax.ShapeDtypeStruct(olds[0].shape, jnp.float32)
+        *news, done = pl.pallas_call(
+            functools.partial(owner_kernel, layout, numel),
+            out_shape=(state,) * 4 + (jax.ShapeDtypeStruct((8, 128), jnp.float32),),
+            in_specs=[SMEM] + [VMEM] * 6,
+            out_specs=(VMEM,) * 5,
+            compiler_params=params,
+        )(owner, squares, received, *olds)
+    with jax.named_scope("gather_x"):
+        copies = pl.pallas_call(
+            copies_kernel,
+            out_shape=jax.ShapeDtypeStruct((XS,) + gathered.shape, jnp.bfloat16),
+            in_specs=[VMEM, VMEM],
+            out_specs=VMEM,
+            compiler_params=params,
+        )(gathered, done)
+        gathered = exchange(copies, "dp", axis_index_groups=along_x)
+    with jax.named_scope("join"):
         weights = pl.pallas_call(
             join_kernel,
             out_shape=jax.ShapeDtypeStruct((1, rows, width), jnp.bfloat16),
@@ -228,16 +262,7 @@
             out_specs=HBM,
             scratch_shapes=[pltpu.SemaphoreType.DMA((replicas,))],
             compiler_params=params,
-        )(gathered)
-    with jax.named_scope("owned"):
-        state = jax.ShapeDtypeStruct(olds[0].shape, jnp.float32)
-        news = pl.pallas_call(
-            functools.partial(owner_kernel, layout, numel),
-            out_shape=(state,) * 4,
-            in_specs=[SMEM, SMEM] + [VMEM] * 6,
-            out_specs=(VMEM,) * 4,
-            compiler_params=params,
-        )(owner, own_index, squares, received, *olds)
+        )(gathered.reshape(replicas, rows, narrow))
     return (weights,) + tuple(new[None, None] for new in news)
 
 

time: 132 us -> 124 us (0.939)
  waiting for transfers between devices: 29.9 us -> 11.8 us
  blocking collectives: 87 us -> 99.9 us
    all_to_all x1, waiting for transfers between devices: 29.9 us -> 11.8 us  [local(): gathered = exchange(copies, 'dp', axis_index_groups=along_y)]
    all_to_all x1 -> x3, blocking collectives: 42.9 us -> 58.1 us  [the longest x1 20.3 us: local(): blocks = exchange(blocks, 'dp', axis_index_groups=along_y)]
    all_to_all x1, blocking collectives: 22.1 us -> 17.5 us  [local(): received = exchange(payload, 'dp')]
    all_to_all x1, blocking collectives: 22 us -> 24.3 us  [local(): squares = exchange(squares, 'section')]
  transfers between devices with their start and end apart: 1 -> 1, of which waited for: 1 -> 1; matrix products, arithmetic and copies ran while one was open for 0% -> 0% of each run, Pallas kernels for 1% -> 2%
where the time goes in v6:
time: 124 us
  blocking collectives  99.9 us (81%)
  waiting for transfers between devices  11.8 us (10%)
  Pallas kernels  5.66 us (5%)
  starting transfers between devices  3.94 us (3%)
  local copies, waits for them, and re-layouts  1.36 us (1%)
    all_to_all x1, blocking collectives, local(): squares = exchange(squares, 'section')  24.3 us
    all_to_all x1, blocking collectives, local(): blocks = exchange(blocks, 'dp', axis_index_groups=along_y)  20.3 us
    all_to_all x1, blocking collectives, local(): gathered = exchange(copies, 'dp', axis_index_groups=along_x)  19.9 us
    all_to_all x1, blocking collectives, local(): blocks = exchange(blocks, 'dp', axis_index_groups=along_x)  17.9 us
    all_to_all x1, blocking collectives, local(): received = exchange(payload, 'dp')  17.5 us
    all_to_all x1, waiting for transfers between devices, local(): gathered = exchange(copies, 'dp', axis_index_groups=along_y)  11.8 us
    all_to_all x1, starting transfers between devices, local(): gathered = exchange(copies, 'dp', axis_index_groups=along_y)  3.94 us
  transfers between devices with their start and end apart: 1, of which 1 were waited for; matrix products, arithmetic and copies ran while one was open for 0% of the time, Pallas kernels for 2%

profile of v6, /device:TPU:1, one launch (start us, length us, event | category | flops | bytes accessed | tf_op | source)
XLA Modules:
  0.0 123.7 jit_solution(4670759056443216537)
XLA Ops:
  0.6 0.0 copy-start
  0.6 1.3 %copy-done = bf16[1,1,80,8192]{3,2,1,0:T(8,128)(2,1)S(1)} copy-done((bf16[1,1,80,8192]{3,2,1,0:T(8,128)(2,1)S(1)}, bf16[1,1,80,8192]{3,2,1,0:T(8,128)(2,1)}, u32[]{:S(2)}) %copy-start) | copy-done | bytes 1310744
  1.9 0.1 reduce_x.1
  2.1 17.9 %all_to_all.30 = bf16[4,80,2048]{2,1,0:T(8,128)(2,1)S(1)} all-to-all(bf16[4,80,2048]{2,1,0:T(8,128)(2,1)S(1)} %reduce_x.1), channel_id=1, replica_groups={{0,8,16,24},{1,9,17,25},{2,10,18,26},{3,11,19,27},{4,12,20,28},{5,13,21..., dimensions={0} | all-to-all | bytes 2621440 | tf_op jit(solution)/shard_map/reduce_x/all_to_all | solution.py:206
  20.0 0.0 copy-start.1
  20.0 0.0 copy-start.2
  20.0 0.0 copy-start.3
  20.0 0.0 copy-start.5
  20.0 0.2 reduce_sum.21
  20.3 20.3 %all_to_all.31.parts = bf16[8,80,256]{2,1,0:T(8,128)(2,1)S(1)} all-to-all(bf16[8,80,256]{2,1,0:T(8,128)(2,1)S(1)} %bitcast.28), channel_id=1, replica_groups={{0,1,2,3,4,5,6,7},{8,9,10,11,12,13,14,15},{16,17,18,19,20,21,22,23},{24..., dimensions={0} | all-to-all | bytes 655360 | tf_op jit(solution)/shard_map/reduce_y/all_to_all | solution.py:210
  40.6 0.0 copy-done.1
  40.6 0.0 copy-done.2
  40.6 0.0 copy-done.3
  40.6 0.0 copy-done.5
  40.6 0.7 split.1
  41.2 0.0 copy-start.4
  41.2 17.5 %all_to_all.32.received = bf16[32,72,128]{2,1,0:T(8,128)(2,1)S(1)} all-to-all(bf16[32,72,128]{2,1,0:T(8,128)(2,1)S(1)} %get-tuple-element.12), channel_id=1, replica_groups=mesh['section'=16,'dp'=32] {'dp'}, dimensions={0} | all-to-all | bytes 1179648 | tf_op jit(solution)/shard_map/to_owners/all_to_all | solution.py:223
  58.8 24.3 %all_to_all.33.squares = f32[16,8,128]{2,1,0:T(8,128)S(1)} all-to-all(f32[16,8,128]{2,1,0:T(8,128)S(1)} %broadcast_in_dim.15), channel_id=1, replica_groups=mesh['section'=16,'dp'=32] {'section'}, dimensions={0} | all-to-all | bytes 131072 | tf_op jit(solution)/shard_map/squares/all_to_all | solution.py:227
  83.1 1.6 %columns.1 = bf16[8,80,256]{2,1,0:T(8,128)(2,1)} custom-call(s32[24]{0:T(128)S(1)} %bitcast.26, f32[16,8,128]{2,1,0:T(8,128)S(1)} %all_to_all.33.squares, f32[80,256]{1,0:T(8,128)S(1)} %get-tuple-element.13.mean, bf16[32,72,128]{2,1,0:T(8,128)(2,1)S(1)} %all_to_all.32.received), custom_call_target="tpu_custom_call" | custom-call | tf_op jit(solution)/shard_map/columns/pallas_call | solution.py:229
  84.6 3.9 %all-to-all-start.4 = ((bf16[8,80,256]{2,1,0:T(8,128)(2,1)}), bf16[8,80,256]{2,1,0:T(8,128)(2,1)S(1)}, u32[]{:S(2)}, u32[]{:S(2)}) async-start(bf16[8,80,256]{2,1,0:T(8,128)(2,1)} %columns.1), calls=%async_computation.4 | async-start | bytes 655360 | tf_op jit(solution)/shard_map/gather_y/all_to_all | solution.py:238
  88.6 0.0 copy-done.4
  88.6 1.9 %owned.1 = (f32[8,8192]{1,0:T(8,128)}, f32[8,8192]{1,0:T(8,128)}, f32[8,8192]{1,0:T(8,128)}, f32[8,8192]{1,0:T(8,128)}, f32[8,128]{1,0:T(8,128)S(1)}) custom-call(s32[24]{0:T(128)S(1)} %bitcast.27, f32[16,8,128]{2,1,0:T(8,128)S(1)} %all_to_all.33.squares, bf16[32,72,128]{2,1,0:T(8,128)(2,1)S(1)} %all_to_all.32.received, f32[8,8192]{1,0:T(8,128)S(1)} %bitcast.19, ...), custom_call_target="tpu_custom_call" | custom-call | tf_op jit(solution)/shard_map/owned/pallas_call | solution.py:241
  90.5 11.8 %all-to-all-done.4.block = bf16[8,80,256]{2,1,0:T(8,128)(2,1)S(1)} async-done(((bf16[8,80,256]{2,1,0:T(8,128)(2,1)}), bf16[8,80,256]{2,1,0:T(8,128)(2,1)S(1)}, u32[]{:S(2)}, u32[]{:S(2)}) %all-to-all-start.4) | async-done | bytes 327712 | tf_op jit(solution)/shard_map/gather_y/all_to_all | solution.py:238
  102.3 0.1 gather_x.1
  102.4 19.9 %all_to_all.34 = bf16[4,8,80,256]{3,2,1,0:T(8,128)(2,1)S(1)} all-to-all(bf16[4,8,80,256]{3,2,1,0:T(8,128)(2,1)S(1)} %gather_x.1), channel_id=1, replica_groups={{0,8,16,24},{1,9,17,25},{2,10,18,26},{3,11,19,27},{4,12,20,28},{5,13,21..., dimensions={0} | all-to-all | bytes 2621440 | tf_op jit(solution)/shard_map/gather_x/all_to_all | solution.py:256
  122.3 1.3 %join.1 = bf16[1,80,8192]{2,1,0:T(8,128)(2,1)} custom-call(bf16[32,80,256]{2,1,0:T(8,128)(2,1)S(1)} %bitcast.17), custom_call_target="tpu_custom_call" | custom-call | tf_op jit(solution)/shard_map/join/pallas_call | solution.py:258
  (3 shorter events, 0.1 us)
Async XLA Ops:
  0.6 1.3 %copy-start = (bf16[1,1,80,8192]{3,2,1,0:T(8,128)(2,1)S(1)}, bf16[1,1,80,8192]{3,2,1,0:T(8,128)(2,1)}, u32[]{:S(2)}) copy-start(bf16[1,1,80,8192]{3,2,1,0:T(8,128)(2,1)} %grads.1) | copy-start | bytes 3932164
  20.0 20.6 %copy-start.1 = (f32[1,1,8,8192]{3,2,1,0:T(8,128)S(1)}, f32[1,1,8,8192]{3,2,1,0:T(8,128)}, u32[]{:S(2)}) copy-start(f32[1,1,8,8192]{3,2,1,0:T(8,128)} %param.8) | copy-start | bytes 786436
  20.0 20.6 %copy-start.2 = (f32[1,1,8,8192]{3,2,1,0:T(8,128)S(1)}, f32[1,1,8,8192]{3,2,1,0:T(8,128)}, u32[]{:S(2)}) copy-start(f32[1,1,8,8192]{3,2,1,0:T(8,128)} %param.9) | copy-start | bytes 786436
  20.0 20.6 %copy-start.3 = (f32[1,1,8,8192]{3,2,1,0:T(8,128)S(1)}, f32[1,1,8,8192]{3,2,1,0:T(8,128)}, u32[]{:S(2)}) copy-start(f32[1,1,8,8192]{3,2,1,0:T(8,128)} %param.10) | copy-start | bytes 786436
  20.0 20.6 %copy-start.5 = (s32[1,24]{1,0:T(1,128)S(1)}, s32[1,24]{1,0:T(1,128)}, u32[]{:S(2)}) copy-start(s32[1,24]{1,0:T(1,128)} %param.7) | copy-start | bytes 292
  41.2 47.4 %copy-start.4 = (f32[1,1,8,8192]{3,2,1,0:T(8,128)S(1)}, f32[1,1,8,8192]{3,2,1,0:T(8,128)}, u32[]{:S(2)}) copy-start(f32[1,1,8,8192]{3,2,1,0:T(8,128)} %param.11) | copy-start | bytes 786436
  84.6 17.7 %all-to-all-start.4 = ((bf16[8,80,256]{2,1,0:T(8,128)(2,1)}), bf16[8,80,256]{2,1,0:T(8,128)(2,1)S(1)}, u32[]{:S(2)}, u32[]{:S(2)}) async-start(bf16[8,80,256]{2,1,0:T(8,128)(2,1)} %columns.1), calls=%async_computation.4 | async-start | bytes 655360 | tf_op jit(solution)/shard_map/gather_y/all_to_all | solution.py:238

commit v7 on v5

--- a/solution.py
+++ b/solution.py
@@ -19,6 +19,14 @@
 
 XS = 4
 YS = 8
+CORES = 2
+
+REDUCE_X = (1, 0, 0)
+REDUCE_Y = (7, 0, 0)
+SPREAD = (15, 0, 0)
+SQUARES = (5, 0, 0)
+GATHER_Y = (6, 0, 0)
+GATHER_X = (2, 0, 0)
 
 
 def tensor_layout(all_rows, slot_rows, layers):
@@ -34,6 +42,49 @@
     return layout
 
 
+def first_of(turn, core, other):
+    return turn[0] + turn[1] * core + turn[2] * other
+
+
+def groups_along(axis, turn, sections):
+    replicas = XS * YS
+    groups = []
+    for section in range(sections):
+        base, core = section * replicas, section % CORES
+        if axis == "x":
+            for y in range(YS):
+                first = first_of(turn, core, y)
+                groups.append([base + (x + first) % XS * YS + y for x in range(XS)])
+        elif axis == "y":
+            for x in range(XS):
+                first = first_of(turn, core, x)
+                groups.append([base + x * YS + (y + first) % YS for y in range(YS)])
+        else:
+            first = first_of(turn, core, 0)
+            groups.append([base + (index + first) % replicas for index in range(replicas)])
+    return groups
+
+
+def place_of(position, axis, turn):
+    core = lax.rem(lax.axis_index("section"), CORES)
+    me = lax.axis_index("dp")
+    size, other = {
+        "x": (XS, lax.rem(me, YS)), "y": (YS, lax.div(me, YS)), "dp": (XS * YS, 0),
+    }[axis]
+    return lax.rem(position + first_of(turn, core, other), size)
+
+
+def near_place(far, near):
+    core = lax.rem(lax.axis_index("section"), CORES)
+    return lax.rem(near + first_of(GATHER_Y, core, place_of(far, "x", GATHER_X)), YS)
+
+
+def position_of(place):
+    core = lax.rem(lax.axis_index("section"), CORES)
+    size = XS * YS
+    return lax.rem(place + size - lax.rem(first_of(SPREAD, core, 0), size), size)
+
+
 def adamw_moments(grad, moment, second, factor):
     clipped = factor * grad
     moment_new = beta_one * moment + (1.0 - beta_one) * clipped
@@ -42,10 +93,8 @@
 
 
 def adamw_master(master, moment_new, second_new, decay):
-    direction = (
-        moment_new
-        / (1.0 - beta_one**STEP)
-        / (jnp.sqrt(second_new / (1.0 - beta_two**STEP)) + epsilon)
+    direction = (moment_new * (1.0 / (1.0 - beta_one**STEP))) / (
+        jnp.sqrt(second_new * (1.0 / (1.0 - beta_two**STEP))) + epsilon
     )
     return master - learn_rate * (direction + decay_rate * decay * master)
 
@@ -73,14 +122,10 @@
     empty = jnp.zeros((16, half), jnp.bfloat16)
     for device in range(replicas):
         payload[device, 0:16, :] = empty
+        start = pl.multiple_of(place_of(device, "dp", SPREAD) * width, width)
         for place, state in enumerate((moment, second, master)):
-            block = jnp.concatenate(
-                [
-                    state[:, device * width : device * width + half],
-                    state[:, device * width + half : (device + 1) * width],
-                ],
-                axis=0,
-            )
+            block = state[:, pl.ds(start, width)]
+            block = jnp.concatenate([block[:, :half], block[:, half:]], axis=0)
             payload[device, 16 * place + 16 : 16 * place + 32, :] = block.astype(jnp.bfloat16)
         payload[device, 64:72, :] = squares
     for tensor, (start, count, flag) in enumerate(layout):
@@ -89,7 +134,7 @@
             block = jnp.concatenate(
                 [block, jnp.zeros((8 - count, width), jnp.float32)], axis=0
             )
-        payload[owner[tensor], 0:16, :] = jnp.concatenate(
+        payload[position_of(owner[tensor]), 0:16, :] = jnp.concatenate(
             [block[:, :half], block[:, half:]], axis=0
         ).astype(jnp.bfloat16)
 
@@ -98,7 +143,7 @@
     factor = clip_factor(jnp.sum(squares[...]), numel)
     half = mean.shape[1] // 2
     for tensor, (start, count, flag) in enumerate(layout):
-        root = owner[tensor]
+        root = position_of(owner[tensor])
         rows = slice(start, start + count)
         for place, state in enumerate((moment, second, master)):
             block = received[root, 16 * place + 16 : 16 * place + 32, :].astype(jnp.float32)
@@ -117,22 +162,27 @@
     weights, master_out, moment_out, second_out, average_out,
     master_new, moment_new, second_new, average_new, weight_sems, state_sems,
 ):
-    parts, _, width = blocks.shape
+    _, _, _, width = blocks.shape
+    parts = received.shape[0]
     moves = []
-    for part in range(parts):
-        moves.append(
-            pltpu.make_async_copy(
-                blocks.at[part], weights.at[0, :, pl.ds(part * width, width)], weight_sems.at[part]
-            )
-        )
-        moves[-1].start()
+    for far in range(XS):
+        for near in range(YS):
+            start = place_of(far, "x", GATHER_X) * YS + near_place(far, near)
+            moves.append(
+                pltpu.make_async_copy(
+                    blocks.at[far, near],
+                    weights.at[0, :, pl.ds(pl.multiple_of(start * width, width), width)],
+                    weight_sems.at[far, near],
+                )
+            )
+            moves[-1].start()
     factor = clip_factor(jnp.sum(squares[...]), numel)
     me = lax.axis_index("dp")
     count = jnp.int32(0)
     flag = jnp.float32(0.0)
-    for tensor, (start, rows, decay) in enumerate(layout):
+    for tensor, (start, height, decay) in enumerate(layout):
         mine = owner[tensor] == me
-        count = jnp.where(mine, rows, count)
+        count = jnp.where(mine, height, count)
         flag = jnp.where(mine, decay, flag)
     used = lax.broadcasted_iota(jnp.int32, (8, width), 0) < count
     pairs = (
@@ -143,7 +193,8 @@
     stretch = parts * width // pieces
     for piece in range(pieces):
         for source in range(piece * parts // pieces, (piece + 1) * parts // pieces):
-            columns = slice(source * width, (source + 1) * width)
+            start = pl.multiple_of(place_of(source, "dp", SPREAD) * width, width)
+            columns = pl.ds(start, width)
             grad = received[source, 0:16, :].astype(jnp.float32)
             grad = jnp.concatenate([grad[0:8], grad[8:16]], axis=1)
             olds = (
@@ -151,10 +202,11 @@
                 second[0, 0, :, columns], average[0, 0, :, columns],
             )
             first, squared = adamw_moments(grad, olds[1], olds[2], factor)
-            whole = adamw_master(olds[0], first, squared, flag)
-            mixed = average_keep * olds[3] + (1.0 - average_keep) * whole
-            for (target, _), new, old in zip(pairs, (whole, first, squared, mixed), olds):
+            stepped = adamw_master(olds[0], first, squared, flag)
+            mixed = average_keep * olds[3] + (1.0 - average_keep) * stepped
+            for (target, _), new, old in zip(pairs, (stepped, first, squared, mixed), olds):
                 target[:, columns] = jnp.where(used, new, old)
+    for piece in range(pieces):
         for place, (source, target) in enumerate(pairs):
             columns = pl.ds(piece * stretch, stretch)
             moves.append(
@@ -169,16 +221,28 @@
 
 def cut_kernel(grads, blocks, sems):
     parts, _, width = blocks.shape
-    moves = [
-        pltpu.make_async_copy(
-            grads.at[0, 0, :, pl.ds(part * width, width)], blocks.at[part], sems.at[part]
+    moves = []
+    for part in range(parts):
+        start = pl.multiple_of(place_of(part, "x", REDUCE_X) * width, width)
+        moves.append(
+            pltpu.make_async_copy(
+                grads.at[0, 0, :, pl.ds(start, width)], blocks.at[part], sems.at[part]
+            )
         )
-        for part in range(parts)
-    ]
-    for move in moves:
-        move.start()
+        moves[-1].start()
     for move in moves:
         move.wait()
+
+
+def sum_kernel(parts, blocks):
+    count, _, width = blocks.shape
+    for position in range(count):
+        start = pl.multiple_of(place_of(position, "y", REDUCE_Y) * width, width)
+        columns = pl.ds(start, width)
+        total = parts[0, :, columns].astype(jnp.float32)
+        for part in range(1, parts.shape[0]):
+            total = total + parts[part, :, columns].astype(jnp.float32)
+        blocks[position] = total.astype(jnp.bfloat16)
 
 
 def copies_kernel(block, copies):
@@ -200,8 +264,15 @@
     sections = lax.axis_size("section")
     numel = sections * rows * width
     owner = owners[0]
-    along_x = [[x * YS + y for x in range(XS)] for y in range(YS)]
-    along_y = [[x * YS + y for y in range(YS)] for x in range(XS)]
+    everyone = ("section", "dp")
+    planes = sections // CORES
+    all_sections = [
+        [
+            (plane + SQUARES[0]) % planes * CORES + core
+            for plane in range(planes)
+            for core in range(CORES)
+        ]
+    ]
     exchange = functools.partial(lax.all_to_all, split_axis=0, concat_axis=0, tiled=True)
     params = pltpu.CompilerParams(vmem_limit_bytes=LIMIT)
     olds = (master[0, 0], moment[0, 0], second[0, 0], average[0, 0])
@@ -211,17 +282,22 @@
     with jax.named_scope("reduce_x"):
         blocks = pl.pallas_call(
             cut_kernel,
-            out_shape=jax.ShapeDtypeStruct((XS, rows, wide), jnp.bfloat16),
+            out_shape=pltpu.VMEM((XS, rows, wide), jnp.bfloat16),
             in_specs=[HBM],
             out_specs=VMEM,
             scratch_shapes=[pltpu.SemaphoreType.DMA((XS,))],
             compiler_params=pltpu.CompilerParams(vmem_limit_bytes=LIMIT),
-        )(grads)
-        blocks = exchange(blocks, "dp", axis_index_groups=along_x)
-        summed = jnp.sum(blocks.astype(jnp.float32), axis=0).astype(jnp.bfloat16)
+        )(pltpu.with_memory_space_constraint(grads, pltpu.HBM))
+        blocks = exchange(blocks, everyone, axis_index_groups=groups_along("x", REDUCE_X, sections))
     with jax.named_scope("reduce_y"):
-        blocks = summed.reshape(rows, YS, narrow).transpose(1, 0, 2)
-        blocks = exchange(blocks, "dp", axis_index_groups=along_y)
+        blocks = pl.pallas_call(
+            sum_kernel,
+            out_shape=jax.ShapeDtypeStruct((YS, rows, narrow), jnp.bfloat16),
+            in_specs=[VMEM],
+            out_specs=VMEM,
+            compiler_params=params,
+        )(blocks)
+        blocks = exchange(blocks, everyone, axis_index_groups=groups_along("y", REDUCE_Y, sections))
     with jax.named_scope("split"):
         mean, payload = pl.pallas_call(
             functools.partial(split_kernel, layout, replicas),
@@ -234,11 +310,11 @@
             compiler_params=params,
         )(owner, blocks, olds[0], olds[1], olds[2])
     with jax.named_scope("to_owners"):
-        received = exchange(payload, "dp")
+        received = exchange(payload, everyone, axis_index_groups=groups_along("dp", SPREAD, sections))
     with jax.named_scope("squares"):
         squares = jnp.sum(received[:, 64:72, :].astype(jnp.float32), axis=0)
         squares = jnp.broadcast_to(squares, (sections,) + squares.shape)
-        squares = exchange(squares, "section")
+        squares = exchange(squares, "section", axis_index_groups=all_sections)
     with jax.named_scope("columns"):
         copies = pl.pallas_call(
             functools.partial(column_kernel, layout, numel),
@@ -249,7 +325,7 @@
             compiler_params=params,
         )(owner, squares, mean, received)
     with jax.named_scope("gather_y"):
-        gathered = exchange(copies, "dp", axis_index_groups=along_y)
+        gathered = exchange(copies, everyone, axis_index_groups=groups_along("y", GATHER_Y, sections))
     with jax.named_scope("gather_x"):
         copies = pl.pallas_call(
             copies_kernel,
@@ -258,7 +334,7 @@
             out_specs=VMEM,
             compiler_params=params,
         )(gathered)
-        gathered = exchange(copies, "dp", axis_index_groups=along_x)
+        gathered = exchange(copies, everyone, axis_index_groups=groups_along("x", GATHER_X, sections))
     with jax.named_scope("finish"):
         outs = pl.pallas_call(
             functools.partial(finish_kernel, layout, numel),
@@ -267,11 +343,11 @@
             in_specs=[SMEM] + [VMEM] * 7,
             out_specs=(HBM,) * 5,
             scratch_shapes=[pltpu.VMEM(master.shape[2:], jnp.float32)] * 4
-            + [pltpu.SemaphoreType.DMA((replicas,)), pltpu.SemaphoreType.DMA((4, 4))],
+            + [pltpu.SemaphoreType.DMA((XS, YS)), pltpu.SemaphoreType.DMA((4, 4))],
             compiler_params=params,
         )(
             owner, squares, received, master, moment, second, average,
-            gathered.reshape(replicas, rows, narrow),
+            gathered,
         )
     return tuple(outs)
 

time: 123 us -> 116 us (0.943)
  the two profiles are of different devices: /device:TPU:1 before, /device:TPU:8 now
where the time goes in v7:
time: 116 us
  blocking collectives  110 us (95%)
  Pallas kernels  5.54 us (5%)
    all_to_all x1, blocking collectives, local(): exchange(blocks, everyone, axis_index_groups=groups_along('x', REDUCE_X,...  21.5 us
    all_to_all x1, blocking collectives, local(): exchange(payload, everyone, axis_index_groups=groups_along('dp', SPREAD,...  20.7 us
    all_to_all x1, blocking collectives, local(): exchange(copies, everyone, axis_index_groups=groups_along('x', GATHER_X,...  19.7 us
    all_to_all x1, blocking collectives, local(): squares = exchange(squares, 'section', axis_index_groups=all_sections)  16.2 us
    all_to_all x1, blocking collectives, local(): exchange(copies, everyone, axis_index_groups=groups_along('y', GATHER_Y,...  15.9 us
    all_to_all x1, blocking collectives, local(): exchange(blocks, everyone, axis_index_groups=groups_along('y', REDUCE_Y,...  15.6 us
    pallas_call x1, Pallas kernels, local(): pl.pallas_call(functools.partial(finish_kernel, layout, numel), out_shape...  2.47 us

profile of v7, /device:TPU:8, one launch (start us, length us, event | category | flops | bytes accessed | tf_op | source)
XLA Modules:
  0.0 116.0 jit_solution(6480876861372176151)
XLA Ops:
  0.6 1.3 %reduce_x.1 = bf16[4,80,2048]{2,1,0:T(8,128)(2,1)S(1)} custom-call(bf16[1,1,80,8192]{3,2,1,0:T(8,128)(2,1)} %grads.1), custom_call_target="tpu_custom_call" | custom-call | tf_op jit(solution)/shard_map/reduce_x/pallas_call | solution.py:283
  1.9 21.5 %all_to_all.30.parts = bf16[4,80,2048]{2,1,0:T(8,128)(2,1)S(1)} all-to-all(bf16[4,80,2048]{2,1,0:T(8,128)(2,1)S(1)} %reduce_x.1), channel_id=1, replica_groups={{8,16,24,0},{9,17,25,1},{10,18,26,2},{11,19,27,3},{12,20,28,4},{13,21,2..., dimensions={0} | all-to-all | bytes 2621440 | tf_op jit(solution)/shard_map/reduce_x/all_to_all | solution.py:291
  23.4 0.0 copy-start
  23.4 0.0 copy-start.1
  23.4 0.0 copy-start.2
  23.4 0.0 copy-start.4
  23.4 0.2 reduce_y.1
  23.6 15.6 %all_to_all.31.parts = bf16[8,80,256]{2,1,0:T(8,128)(2,1)S(1)} all-to-all(bf16[8,80,256]{2,1,0:T(8,128)(2,1)S(1)} %reduce_y.1), channel_id=1, replica_groups={{7,0,1,2,3,4,5,6},{15,8,9,10,11,12,13,14},{23,16,17,18,19,20,21,22},{31..., dimensions={0} | all-to-all | bytes 655360 | tf_op jit(solution)/shard_map/reduce_y/all_to_all | solution.py:300
  39.3 0.0 copy-done
  39.3 0.0 copy-done.1
  39.3 0.0 copy-done.2
  39.3 0.0 copy-done.4
  39.3 0.7 split.1
  39.9 20.7 %all_to_all.32.received = bf16[32,72,128]{2,1,0:T(8,128)(2,1)S(1)} all-to-all(bf16[32,72,128]{2,1,0:T(8,128)(2,1)S(1)} %get-tuple-element.7), channel_id=1, replica_groups={{15,16,17,18,19,20,21,22,23,24,25,26,27,28,29,30,31,0,1,2,3,4,5,6,7,8,9..., dimensions={0} | all-to-all | bytes 1179648 | tf_op jit(solution)/shard_map/to_owners/all_to_all | solution.py:313
  60.7 16.2 %all_to_all.33.squares = f32[16,8,128]{2,1,0:T(8,128)S(1)} all-to-all(f32[16,8,128]{2,1,0:T(8,128)S(1)} %broadcast_in_dim.3), channel_id=1, replica_groups={{320,352,384,416,448,480,0,32,64,96,128,160,192,224,256,288},{321,353,3..., dimensions={0} | all-to-all | bytes 131072 | tf_op jit(solution)/shard_map/squares/all_to_all | solution.py:317
  76.9 0.9 columns.1
  77.8 15.9 %all_to_all.34.block = bf16[8,80,256]{2,1,0:T(8,128)(2,1)S(1)} all-to-all(bf16[8,80,256]{2,1,0:T(8,128)(2,1)S(1)} %columns.1), channel_id=1, replica_groups={{6,7,0,1,2,3,4,5},{14,15,8,9,10,11,12,13},{22,23,16,17,18,19,20,21},{30..., dimensions={0} | all-to-all | bytes 655360 | tf_op jit(solution)/shard_map/gather_y/all_to_all | solution.py:328
  93.7 0.1 gather_x.1
  93.8 0.0 copy-start.3
  93.8 19.7 %all_to_all.35.blocks = bf16[4,8,80,256]{3,2,1,0:T(8,128)(2,1)S(1)} all-to-all(bf16[4,8,80,256]{3,2,1,0:T(8,128)(2,1)S(1)} %gather_x.1), channel_id=1, replica_groups={{16,24,0,8},{17,25,1,9},{18,26,2,10},{19,27,3,11},{20,28,4,12},{21,29,5..., dimensions={0} | all-to-all | bytes 2621440 | tf_op jit(solution)/shard_map/gather_x/all_to_all | solution.py:337
  113.5 0.0 copy-done.3
  113.5 2.5 %finish.1 = (bf16[1,80,8192]{2,1,0:T(8,128)(2,1)}, f32[1,1,8,8192]{3,2,1,0:T(8,128)}, f32[1,1,8,8192]{3,2,1,0:T(8,128)}, f32[1,1,8,8192]{3,2,1,0:T(8,128)}, f32[1,1,8,8192]{3,2,1,0:T(8,128)}) custom-call(s32[24]{0:T(128)S(1)} %bitcast.9, f32[16,8,128]{2,1,0:T(8,128)S(1)} %all_to_all.33.squares, bf16[32,72,128]{2,1,0:T(8,128)(2,1)S(1)} %all_to_all.32.received, ...), custom_call_target="tpu_custom_call" | custom-call | tf_op jit(solution)/shard_map/finish/pallas_call | solution.py:339
  (2 shorter events, 0.0 us)
Async XLA Ops:
  23.4 15.8 %copy-start = (f32[1,1,8,8192]{3,2,1,0:T(8,128)S(1)}, f32[1,1,8,8192]{3,2,1,0:T(8,128)}, u32[]{:S(2)}) copy-start(f32[1,1,8,8192]{3,2,1,0:T(8,128)} %master.1) | copy-start | bytes 786436
  23.4 15.8 %copy-start.1 = (f32[1,1,8,8192]{3,2,1,0:T(8,128)S(1)}, f32[1,1,8,8192]{3,2,1,0:T(8,128)}, u32[]{:S(2)}) copy-start(f32[1,1,8,8192]{3,2,1,0:T(8,128)} %moment.1) | copy-start | bytes 786436
  23.4 15.8 %copy-start.2 = (f32[1,1,8,8192]{3,2,1,0:T(8,128)S(1)}, f32[1,1,8,8192]{3,2,1,0:T(8,128)}, u32[]{:S(2)}) copy-start(f32[1,1,8,8192]{3,2,1,0:T(8,128)} %second.1) | copy-start | bytes 786436
  23.4 15.8 %copy-start.4 = (s32[1,24]{1,0:T(1,128)S(1)}, s32[1,24]{1,0:T(1,128)}, u32[]{:S(2)}) copy-start(s32[1,24]{1,0:T(1,128)} %param.7) | copy-start | bytes 292
  93.8 19.7 %copy-start.3 = (f32[1,1,8,8192]{3,2,1,0:T(8,128)S(1)}, f32[1,1,8,8192]{3,2,1,0:T(8,128)}, u32[]{:S(2)}) copy-start(f32[1,1,8,8192]{3,2,1,0:T(8,128)} %average.1) | copy-start | bytes 786436

commit v8 on v7

--- a/solution.py
+++ b/solution.py
@@ -21,12 +21,12 @@
 YS = 8
 CORES = 2
 
-REDUCE_X = (1, 0, 0)
-REDUCE_Y = (7, 0, 0)
-SPREAD = (15, 0, 0)
-SQUARES = (5, 0, 0)
-GATHER_Y = (6, 0, 0)
-GATHER_X = (2, 0, 0)
+REDUCE_X = (1, 0, 0, -1)
+REDUCE_Y = (6, 0, 0, 1)
+SPREAD = (14, 0, 0, 1)
+SQUARES = (5, 0, 0, -1)
+GATHER_Y = (5, 0, 0, 1)
+GATHER_X = (2, 0, 0, -1)
 
 
 def tensor_layout(all_rows, slot_rows, layers):
@@ -54,14 +54,14 @@
         if axis == "x":
             for y in range(YS):
                 first = first_of(turn, core, y)
-                groups.append([base + (x + first) % XS * YS + y for x in range(XS)])
+                groups.append([base + (turn[3] * x + first) % XS * YS + y for x in range(XS)])
         elif axis == "y":
             for x in range(XS):
                 first = first_of(turn, core, x)
-                groups.append([base + x * YS + (y + first) % YS for y in range(YS)])
+                groups.append([base + x * YS + (turn[3] * y + first) % YS for y in range(YS)])
         else:
             first = first_of(turn, core, 0)
-            groups.append([base + (index + first) % replicas for index in range(replicas)])
+            groups.append([base + (turn[3] * index + first) % replicas for index in range(replicas)])
     return groups
 
 
@@ -71,18 +71,18 @@
     size, other = {
         "x": (XS, lax.rem(me, YS)), "y": (YS, lax.div(me, YS)), "dp": (XS * YS, 0),
     }[axis]
-    return lax.rem(position + first_of(turn, core, other), size)
+    return lax.rem(size + turn[3] * position + first_of(turn, core, other), size)
 
 
 def near_place(far, near):
     core = lax.rem(lax.axis_index("section"), CORES)
-    return lax.rem(near + first_of(GATHER_Y, core, place_of(far, "x", GATHER_X)), YS)
+    return lax.rem(YS + GATHER_Y[3] * near + first_of(GATHER_Y, core, place_of(far, "x", GATHER_X)), YS)
 
 
 def position_of(place):
     core = lax.rem(lax.axis_index("section"), CORES)
     size = XS * YS
-    return lax.rem(place + size - lax.rem(first_of(SPREAD, core, 0), size), size)
+    return lax.rem(size + SPREAD[3] * (place - lax.rem(first_of(SPREAD, core, 0), size)), size)
 
 
 def adamw_moments(grad, moment, second, factor):
@@ -268,7 +268,7 @@
     planes = sections // CORES
     all_sections = [
         [
-            (plane + SQUARES[0]) % planes * CORES + core
+            (SQUARES[3] * plane + SQUARES[0]) % planes * CORES + core
             for plane in range(planes)
             for core in range(CORES)
         ]

time: 116 us -> 115 us (level)
  the two profiles are of different devices: /device:TPU:8 before, /device:TPU:1 now
where the time goes in v8:
time: 115 us; the launch traced here: 113 us
  blocking collectives  107 us (93%)
  Pallas kernels  5.54 us (5%)
    all_to_all x1, blocking collectives, local(): squares = exchange(squares, 'section', axis_index_groups=all_sections)  21.2 us
    all_to_all x1, blocking collectives, local(): exchange(payload, everyone, axis_index_groups=groups_along('dp', SPREAD,...  19.5 us
    all_to_all x1, blocking collectives, local(): exchange(blocks, everyone, axis_index_groups=groups_along('x', REDUCE_X,...  17.1 us
    all_to_all x1, blocking collectives, local(): exchange(copies, everyone, axis_index_groups=groups_along('x', GATHER_X,...  17.1 us
    all_to_all x1, blocking collectives, local(): exchange(blocks, everyone, axis_index_groups=groups_along('y', REDUCE_Y,...  17 us
    all_to_all x1, blocking collectives, local(): exchange(copies, everyone, axis_index_groups=groups_along('y', GATHER_Y,...  14.8 us
    pallas_call x1, Pallas kernels, local(): pl.pallas_call(functools.partial(finish_kernel, layout, numel), out_shape...  2.47 us

profile of v8, /device:TPU:1, one launch (start us, length us, event | category | flops | bytes accessed | tf_op | source)
XLA Modules:
  0.0 112.9 jit_solution(2259324161538498548)
XLA Ops:
  0.6 1.3 %reduce_x.1 = bf16[4,80,2048]{2,1,0:T(8,128)(2,1)S(1)} custom-call(bf16[1,1,80,8192]{3,2,1,0:T(8,128)(2,1)} %grads.1), custom_call_target="tpu_custom_call" | custom-call | tf_op jit(solution)/shard_map/reduce_x/pallas_call | solution.py:283
  1.9 17.1 %all_to_all.30.parts = bf16[4,80,2048]{2,1,0:T(8,128)(2,1)S(1)} all-to-all(bf16[4,80,2048]{2,1,0:T(8,128)(2,1)S(1)} %reduce_x.1), channel_id=1, replica_groups={{8,0,24,16},{9,1,25,17},{10,2,26,18},{11,3,27,19},{12,4,28,20},{13,5,29..., dimensions={0} | all-to-all | bytes 2621440 | tf_op jit(solution)/shard_map/reduce_x/all_to_all | solution.py:291
  19.1 0.0 copy-start
  19.1 0.0 copy-start.1
  19.1 0.0 copy-start.2
  19.1 0.0 copy-start.4
  19.1 0.2 reduce_y.1
  19.3 17.0 %all_to_all.31.parts = bf16[8,80,256]{2,1,0:T(8,128)(2,1)S(1)} all-to-all(bf16[8,80,256]{2,1,0:T(8,128)(2,1)S(1)} %reduce_y.1), channel_id=1, replica_groups={{6,7,0,1,2,3,4,5},{14,15,8,9,10,11,12,13},{22,23,16,17,18,19,20,21},{30..., dimensions={0} | all-to-all | bytes 655360 | tf_op jit(solution)/shard_map/reduce_y/all_to_all | solution.py:300
  36.2 0.0 copy-done
  36.2 0.0 copy-done.1
  36.2 0.0 copy-done.2
  36.2 0.0 copy-done.4
  36.2 0.7 split.1
  36.9 19.5 %all_to_all.32.received = bf16[32,72,128]{2,1,0:T(8,128)(2,1)S(1)} all-to-all(bf16[32,72,128]{2,1,0:T(8,128)(2,1)S(1)} %get-tuple-element.7), channel_id=1, replica_groups={{14,15,16,17,18,19,20,21,22,23,24,25,26,27,28,29,30,31,0,1,2,3,4,5,6,7,..., dimensions={0} | all-to-all | bytes 1179648 | tf_op jit(solution)/shard_map/to_owners/all_to_all | solution.py:313
  56.5 21.2 %all_to_all.33.squares = f32[16,8,128]{2,1,0:T(8,128)S(1)} all-to-all(f32[16,8,128]{2,1,0:T(8,128)S(1)} %broadcast_in_dim.3), channel_id=1, replica_groups={{320,352,256,288,192,224,128,160,64,96,0,32,448,480,384,416},{321,353,2..., dimensions={0} | all-to-all | bytes 131072 | tf_op jit(solution)/shard_map/squares/all_to_all | solution.py:317
  77.6 0.9 columns.1
  78.5 14.8 %all_to_all.34.block = bf16[8,80,256]{2,1,0:T(8,128)(2,1)S(1)} all-to-all(bf16[8,80,256]{2,1,0:T(8,128)(2,1)S(1)} %columns.1), channel_id=1, replica_groups={{5,6,7,0,1,2,3,4},{13,14,15,8,9,10,11,12},{21,22,23,16,17,18,19,20},{29..., dimensions={0} | all-to-all | bytes 655360 | tf_op jit(solution)/shard_map/gather_y/all_to_all | solution.py:328
  93.3 0.1 gather_x.1
  93.4 0.0 copy-start.3
  93.4 17.1 %all_to_all.35.blocks = bf16[4,8,80,256]{3,2,1,0:T(8,128)(2,1)S(1)} all-to-all(bf16[4,8,80,256]{3,2,1,0:T(8,128)(2,1)S(1)} %gather_x.1), channel_id=1, replica_groups={{16,8,0,24},{17,9,1,25},{18,10,2,26},{19,11,3,27},{20,12,4,28},{21,13,5..., dimensions={0} | all-to-all | bytes 2621440 | tf_op jit(solution)/shard_map/gather_x/all_to_all | solution.py:337
  110.4 0.0 copy-done.3
  110.5 2.5 %finish.1 = (bf16[1,80,8192]{2,1,0:T(8,128)(2,1)}, f32[1,1,8,8192]{3,2,1,0:T(8,128)}, f32[1,1,8,8192]{3,2,1,0:T(8,128)}, f32[1,1,8,8192]{3,2,1,0:T(8,128)}, f32[1,1,8,8192]{3,2,1,0:T(8,128)}) custom-call(s32[24]{0:T(128)S(1)} %bitcast.9, f32[16,8,128]{2,1,0:T(8,128)S(1)} %all_to_all.33.squares, bf16[32,72,128]{2,1,0:T(8,128)(2,1)S(1)} %all_to_all.32.received, ...), custom_call_target="tpu_custom_call" | custom-call | tf_op jit(solution)/shard_map/finish/pallas_call | solution.py:339
  (2 shorter events, 0.0 us)
Async XLA Ops:
  19.1 17.1 %copy-start = (f32[1,1,8,8192]{3,2,1,0:T(8,128)S(1)}, f32[1,1,8,8192]{3,2,1,0:T(8,128)}, u32[]{:S(2)}) copy-start(f32[1,1,8,8192]{3,2,1,0:T(8,128)} %master.1) | copy-start | bytes 786436
  19.1 17.1 %copy-start.1 = (f32[1,1,8,8192]{3,2,1,0:T(8,128)S(1)}, f32[1,1,8,8192]{3,2,1,0:T(8,128)}, u32[]{:S(2)}) copy-start(f32[1,1,8,8192]{3,2,1,0:T(8,128)} %moment.1) | copy-start | bytes 786436
  19.1 17.1 %copy-start.2 = (f32[1,1,8,8192]{3,2,1,0:T(8,128)S(1)}, f32[1,1,8,8192]{3,2,1,0:T(8,128)}, u32[]{:S(2)}) copy-start(f32[1,1,8,8192]{3,2,1,0:T(8,128)} %second.1) | copy-start | bytes 786436
  19.1 17.1 %copy-start.4 = (s32[1,24]{1,0:T(1,128)S(1)}, s32[1,24]{1,0:T(1,128)}, u32[]{:S(2)}) copy-start(s32[1,24]{1,0:T(1,128)} %param.7) | copy-start | bytes 292
  93.4 17.1 %copy-start.3 = (f32[1,1,8,8192]{3,2,1,0:T(8,128)S(1)}, f32[1,1,8,8192]{3,2,1,0:T(8,128)}, u32[]{:S(2)}) copy-start(f32[1,1,8,8192]{3,2,1,0:T(8,128)} %average.1) | copy-start | bytes 786436

commit v9 on v8

--- a/solution.py
+++ b/solution.py
@@ -23,7 +23,7 @@
 
 REDUCE_X = (1, 0, 0, -1)
 REDUCE_Y = (6, 0, 0, 1)
-SPREAD = (14, 0, 0, 1)
+SPREAD = (15, 0, 0, 1)
 SQUARES = (5, 0, 0, -1)
 GATHER_Y = (5, 0, 0, 1)
 GATHER_X = (2, 0, 0, -1)
@@ -312,8 +312,8 @@
     with jax.named_scope("to_owners"):
         received = exchange(payload, everyone, axis_index_groups=groups_along("dp", SPREAD, sections))
     with jax.named_scope("squares"):
-        squares = jnp.sum(received[:, 64:72, :].astype(jnp.float32), axis=0)
-        squares = jnp.broadcast_to(squares, (sections,) + squares.shape)
+        squares = jnp.sum(received[:, 64:72, :].astype(jnp.float32), axis=(0, 1))
+        squares = jnp.broadcast_to(squares, (sections, 1) + squares.shape)
         squares = exchange(squares, "section", axis_index_groups=all_sections)
     with jax.named_scope("columns"):
         copies = pl.pallas_call(

time: 115 us -> 114 us (level)
  no operation moved by 1% of the time
where the time goes in v9:
time: 114 us; the launch traced here: 112 us
  blocking collectives  106 us (93%)
  Pallas kernels  5.54 us (5%)
    all_to_all x1, blocking collectives, local(): squares = exchange(squares, 'section', axis_index_groups=all_sections)  20.9 us
    all_to_all x1, blocking collectives, local(): exchange(payload, everyone, axis_index_groups=groups_along('dp', SPREAD,...  18.9 us
    all_to_all x1, blocking collectives, local(): exchange(copies, everyone, axis_index_groups=groups_along('x', GATHER_X,...  17.8 us
    all_to_all x1, blocking collectives, local(): exchange(blocks, everyone, axis_index_groups=groups_along('x', REDUCE_X,...  17.1 us
    all_to_all x1, blocking collectives, local(): exchange(blocks, everyone, axis_index_groups=groups_along('y', REDUCE_Y,...  17 us
    all_to_all x1, blocking collectives, local(): exchange(copies, everyone, axis_index_groups=groups_along('y', GATHER_Y,...  13.9 us
    pallas_call x1, Pallas kernels, local(): pl.pallas_call(functools.partial(finish_kernel, layout, numel), out_shape...  2.47 us

profile of v9, /device:TPU:1, one launch (start us, length us, event | category | flops | bytes accessed | tf_op | source)
XLA Modules:
  0.0 111.8 jit_solution(2352085955383225659)
XLA Ops:
  0.6 1.3 %reduce_x.1 = bf16[4,80,2048]{2,1,0:T(8,128)(2,1)S(1)} custom-call(bf16[1,1,80,8192]{3,2,1,0:T(8,128)(2,1)} %grads.1), custom_call_target="tpu_custom_call" | custom-call | tf_op jit(solution)/shard_map/reduce_x/pallas_call | solution.py:283
  1.9 17.1 %all_to_all.30.parts = bf16[4,80,2048]{2,1,0:T(8,128)(2,1)S(1)} all-to-all(bf16[4,80,2048]{2,1,0:T(8,128)(2,1)S(1)} %reduce_x.1), channel_id=1, replica_groups={{8,0,24,16},{9,1,25,17},{10,2,26,18},{11,3,27,19},{12,4,28,20},{13,5,29..., dimensions={0} | all-to-all | bytes 2621440 | tf_op jit(solution)/shard_map/reduce_x/all_to_all | solution.py:291
  19.1 0.0 copy-start
  19.1 0.0 copy-start.1
  19.1 0.0 copy-start.2
  19.1 0.0 copy-start.4
  19.1 0.2 reduce_y.1
  19.3 17.0 %all_to_all.31.parts = bf16[8,80,256]{2,1,0:T(8,128)(2,1)S(1)} all-to-all(bf16[8,80,256]{2,1,0:T(8,128)(2,1)S(1)} %reduce_y.1), channel_id=1, replica_groups={{6,7,0,1,2,3,4,5},{14,15,8,9,10,11,12,13},{22,23,16,17,18,19,20,21},{30..., dimensions={0} | all-to-all | bytes 655360 | tf_op jit(solution)/shard_map/reduce_y/all_to_all | solution.py:300
  36.2 0.0 copy-done
  36.2 0.0 copy-done.1
  36.2 0.0 copy-done.2
  36.2 0.0 copy-done.4
  36.2 0.7 split.1
  36.9 18.9 %all_to_all.32.received = bf16[32,72,128]{2,1,0:T(8,128)(2,1)S(1)} all-to-all(bf16[32,72,128]{2,1,0:T(8,128)(2,1)S(1)} %get-tuple-element.7), channel_id=1, replica_groups={{15,16,17,18,19,20,21,22,23,24,25,26,27,28,29,30,31,0,1,2,3,4,5,6,7,8,9..., dimensions={0} | all-to-all | bytes 1179648 | tf_op jit(solution)/shard_map/to_owners/all_to_all | solution.py:313
  55.8 0.1 convert_reduce_fusion
  55.9 20.9 %all_to_all.33.squares = f32[16,1,128]{2,1,0:T(1,128)S(1)} all-to-all(f32[16,1,128]{2,1,0:T(1,128)S(1)} %broadcast_in_dim.3), channel_id=1, replica_groups={{320,352,256,288,192,224,128,160,64,96,0,32,448,480,384,416},{321,353,2..., dimensions={0} | all-to-all | bytes 16384 | tf_op jit(solution)/shard_map/squares/all_to_all | solution.py:317
  76.7 0.9 columns.1
  77.6 13.9 %all_to_all.34.block = bf16[8,80,256]{2,1,0:T(8,128)(2,1)S(1)} all-to-all(bf16[8,80,256]{2,1,0:T(8,128)(2,1)S(1)} %columns.1), channel_id=1, replica_groups={{5,6,7,0,1,2,3,4},{13,14,15,8,9,10,11,12},{21,22,23,16,17,18,19,20},{29..., dimensions={0} | all-to-all | bytes 655360 | tf_op jit(solution)/shard_map/gather_y/all_to_all | solution.py:328
  91.5 0.1 gather_x.1
  91.6 0.0 copy-start.3
  91.6 17.8 %all_to_all.35.blocks = bf16[4,8,80,256]{3,2,1,0:T(8,128)(2,1)S(1)} all-to-all(bf16[4,8,80,256]{3,2,1,0:T(8,128)(2,1)S(1)} %gather_x.1), channel_id=1, replica_groups={{16,8,0,24},{17,9,1,25},{18,10,2,26},{19,11,3,27},{20,12,4,28},{21,13,5..., dimensions={0} | all-to-all | bytes 2621440 | tf_op jit(solution)/shard_map/gather_x/all_to_all | solution.py:337
  109.3 0.0 copy-done.3
  109.3 2.5 %finish.1 = (bf16[1,80,8192]{2,1,0:T(8,128)(2,1)}, f32[1,1,8,8192]{3,2,1,0:T(8,128)}, f32[1,1,8,8192]{3,2,1,0:T(8,128)}, f32[1,1,8,8192]{3,2,1,0:T(8,128)}, f32[1,1,8,8192]{3,2,1,0:T(8,128)}) custom-call(s32[24]{0:T(128)S(1)} %bitcast.9, f32[16,1,128]{2,1,0:T(1,128)S(1)} %all_to_all.33.squares, bf16[32,72,128]{2,1,0:T(8,128)(2,1)S(1)} %all_to_all.32.received, ...), custom_call_target="tpu_custom_call" | custom-call | tf_op jit(solution)/shard_map/finish/pallas_call | solution.py:339
  (1 shorter events, 0.0 us)
Async XLA Ops:
  19.1 17.1 %copy-start = (f32[1,1,8,8192]{3,2,1,0:T(8,128)S(1)}, f32[1,1,8,8192]{3,2,1,0:T(8,128)}, u32[]{:S(2)}) copy-start(f32[1,1,8,8192]{3,2,1,0:T(8,128)} %master.1) | copy-start | bytes 786436
  19.1 17.1 %copy-start.1 = (f32[1,1,8,8192]{3,2,1,0:T(8,128)S(1)}, f32[1,1,8,8192]{3,2,1,0:T(8,128)}, u32[]{:S(2)}) copy-start(f32[1,1,8,8192]{3,2,1,0:T(8,128)} %moment.1) | copy-start | bytes 786436
  19.1 17.1 %copy-start.2 = (f32[1,1,8,8192]{3,2,1,0:T(8,128)S(1)}, f32[1,1,8,8192]{3,2,1,0:T(8,128)}, u32[]{:S(2)}) copy-start(f32[1,1,8,8192]{3,2,1,0:T(8,128)} %second.1) | copy-start | bytes 786436
  19.1 17.1 %copy-start.4 = (s32[1,24]{1,0:T(1,128)S(1)}, s32[1,24]{1,0:T(1,128)}, u32[]{:S(2)}) copy-start(s32[1,24]{1,0:T(1,128)} %param.7) | copy-start | bytes 292
  91.6 17.8 %copy-start.3 = (f32[1,1,8,8192]{3,2,1,0:T(8,128)S(1)}, f32[1,1,8,8192]{3,2,1,0:T(8,128)}, u32[]{:S(2)}) copy-start(f32[1,1,8,8192]{3,2,1,0:T(8,128)} %average.1) | copy-start | bytes 786436

commit v10 on v9

--- a/solution.py
+++ b/solution.py
@@ -160,22 +160,27 @@
 def finish_kernel(
     layout, numel, owner, squares, received, master, moment, second, average, blocks,
     weights, master_out, moment_out, second_out, average_out,
-    master_new, moment_new, second_new, average_new, weight_sems, state_sems,
+    whole, master_new, moment_new, second_new, average_new, weight_sems, state_sems,
 ):
     _, _, _, width = blocks.shape
     parts = received.shape[0]
     moves = []
-    for far in range(XS):
-        for near in range(YS):
-            start = place_of(far, "x", GATHER_X) * YS + near_place(far, near)
-            moves.append(
-                pltpu.make_async_copy(
-                    blocks.at[far, near],
-                    weights.at[0, :, pl.ds(pl.multiple_of(start * width, width), width)],
-                    weight_sems.at[far, near],
-                )
-            )
-            moves[-1].start()
+    starts = [
+        (far, near, place_of(far, "x", GATHER_X) * YS + near_place(far, near))
+        for far in range(XS)
+        for near in range(YS)
+    ]
+    for row in range(0, whole.shape[0], 16):
+        stripe = slice(row, row + 16)
+        for far, near, start in starts:
+            columns = pl.ds(pl.multiple_of(start * width, width), width)
+            whole[stripe, columns] = blocks[far, near, stripe, :]
+        moves.append(
+            pltpu.make_async_copy(
+                whole.at[pl.ds(row, 16)], weights.at[0, pl.ds(row, 16)], weight_sems.at[row // 16]
+            )
+        )
+        moves[-1].start()
     factor = clip_factor(jnp.sum(squares[...]), numel)
     me = lax.axis_index("dp")
     count = jnp.int32(0)
@@ -269,8 +274,8 @@
     all_sections = [
         [
             (SQUARES[3] * plane + SQUARES[0]) % planes * CORES + core
+            for core in range(CORES)
             for plane in range(planes)
-            for core in range(CORES)
         ]
     ]
     exchange = functools.partial(lax.all_to_all, split_axis=0, concat_axis=0, tiled=True)
@@ -342,8 +347,9 @@
             + (jax.ShapeDtypeStruct(master.shape, jnp.float32),) * 4,
             in_specs=[SMEM] + [VMEM] * 7,
             out_specs=(HBM,) * 5,
-            scratch_shapes=[pltpu.VMEM(master.shape[2:], jnp.float32)] * 4
-            + [pltpu.SemaphoreType.DMA((XS, YS)), pltpu.SemaphoreType.DMA((4, 4))],
+            scratch_shapes=[pltpu.VMEM((rows, width), jnp.bfloat16)]
+            + [pltpu.VMEM(master.shape[2:], jnp.float32)] * 4
+            + [pltpu.SemaphoreType.DMA((rows // 16,)), pltpu.SemaphoreType.DMA((4, 4))],
             compiler_params=params,
         )(
             owner, squares, received, master, moment, second, average,

time: 114 us -> 114 us (level)
  no operation moved by 1% of the time
where the time goes in v10:
time: 114 us; the launch traced here: 112 us
  blocking collectives  105 us (92%)
  Pallas kernels  5.65 us (5%)
    all_to_all x1, blocking collectives, local(): squares = exchange(squares, 'section', axis_index_groups=all_sections)  20.9 us
    all_to_all x1, blocking collectives, local(): exchange(payload, everyone, axis_index_groups=groups_along('dp', SPREAD,...  18.9 us
    all_to_all x1, blocking collectives, local(): exchange(copies, everyone, axis_index_groups=groups_along('x', GATHER_X,...  17.8 us
    all_to_all x1, blocking collectives, local(): exchange(blocks, everyone, axis_index_groups=groups_along('x', REDUCE_X,...  17.1 us
    all_to_all x1, blocking collectives, local(): exchange(blocks, everyone, axis_index_groups=groups_along('y', REDUCE_Y,...  17 us
    all_to_all x1, blocking collectives, local(): exchange(copies, everyone, axis_index_groups=groups_along('y', GATHER_Y,...  13.9 us
    pallas_call x1, Pallas kernels, local(): pl.pallas_call(functools.partial(finish_kernel, layout, numel), out_shape...  2.58 us

profile of v10, /device:TPU:1, one launch (start us, length us, event | category | flops | bytes accessed | tf_op | source)
XLA Modules:
  0.0 111.9 jit_solution(5587098018964881934)
XLA Ops:
  0.6 1.3 %reduce_x.1 = bf16[4,80,2048]{2,1,0:T(8,128)(2,1)S(1)} custom-call(bf16[1,1,80,8192]{3,2,1,0:T(8,128)(2,1)} %grads.1), custom_call_target="tpu_custom_call" | custom-call | tf_op jit(solution)/shard_map/reduce_x/pallas_call | solution.py:288
  1.9 17.1 %all_to_all.30.parts = bf16[4,80,2048]{2,1,0:T(8,128)(2,1)S(1)} all-to-all(bf16[4,80,2048]{2,1,0:T(8,128)(2,1)S(1)} %reduce_x.1), channel_id=1, replica_groups={{8,0,24,16},{9,1,25,17},{10,2,26,18},{11,3,27,19},{12,4,28,20},{13,5,29..., dimensions={0} | all-to-all | bytes 2621440 | tf_op jit(solution)/shard_map/reduce_x/all_to_all | solution.py:296
  19.1 0.0 copy-start
  19.1 0.0 copy-start.1
  19.1 0.0 copy-start.2
  19.1 0.0 copy-start.4
  19.1 0.2 reduce_y.1
  19.3 17.0 %all_to_all.31.parts = bf16[8,80,256]{2,1,0:T(8,128)(2,1)S(1)} all-to-all(bf16[8,80,256]{2,1,0:T(8,128)(2,1)S(1)} %reduce_y.1), channel_id=1, replica_groups={{6,7,0,1,2,3,4,5},{14,15,8,9,10,11,12,13},{22,23,16,17,18,19,20,21},{30..., dimensions={0} | all-to-all | bytes 655360 | tf_op jit(solution)/shard_map/reduce_y/all_to_all | solution.py:305
  36.2 0.0 copy-done
  36.2 0.0 copy-done.1
  36.2 0.0 copy-done.2
  36.2 0.0 copy-done.4
  36.2 0.7 split.1
  36.9 18.9 %all_to_all.32.received = bf16[32,72,128]{2,1,0:T(8,128)(2,1)S(1)} all-to-all(bf16[32,72,128]{2,1,0:T(8,128)(2,1)S(1)} %get-tuple-element.7), channel_id=1, replica_groups={{15,16,17,18,19,20,21,22,23,24,25,26,27,28,29,30,31,0,1,2,3,4,5,6,7,8,9..., dimensions={0} | all-to-all | bytes 1179648 | tf_op jit(solution)/shard_map/to_owners/all_to_all | solution.py:318
  55.8 0.1 convert_reduce_fusion
  55.9 20.9 %all_to_all.33.squares = f32[16,1,128]{2,1,0:T(1,128)S(1)} all-to-all(f32[16,1,128]{2,1,0:T(1,128)S(1)} %broadcast_in_dim.3), channel_id=1, replica_groups={{320,256,192,128,64,0,448,384,352,288,224,160,96,32,480,416},{321,257,1..., dimensions={0} | all-to-all | bytes 16384 | tf_op jit(solution)/shard_map/squares/all_to_all | solution.py:322
  76.7 0.9 columns.1
  77.6 13.9 %all_to_all.34.block = bf16[8,80,256]{2,1,0:T(8,128)(2,1)S(1)} all-to-all(bf16[8,80,256]{2,1,0:T(8,128)(2,1)S(1)} %columns.1), channel_id=1, replica_groups={{5,6,7,0,1,2,3,4},{13,14,15,8,9,10,11,12},{21,22,23,16,17,18,19,20},{29..., dimensions={0} | all-to-all | bytes 655360 | tf_op jit(solution)/shard_map/gather_y/all_to_all | solution.py:333
  91.5 0.1 gather_x.1
  91.6 0.0 copy-start.3
  91.6 17.8 %all_to_all.35.blocks = bf16[4,8,80,256]{3,2,1,0:T(8,128)(2,1)S(1)} all-to-all(bf16[4,8,80,256]{3,2,1,0:T(8,128)(2,1)S(1)} %gather_x.1), channel_id=1, replica_groups={{16,8,0,24},{17,9,1,25},{18,10,2,26},{19,11,3,27},{20,12,4,28},{21,13,5..., dimensions={0} | all-to-all | bytes 2621440 | tf_op jit(solution)/shard_map/gather_x/all_to_all | solution.py:342
  109.3 0.0 copy-done.3
  109.3 2.6 %finish.1 = (bf16[1,80,8192]{2,1,0:T(8,128)(2,1)}, f32[1,1,8,8192]{3,2,1,0:T(8,128)}, f32[1,1,8,8192]{3,2,1,0:T(8,128)}, f32[1,1,8,8192]{3,2,1,0:T(8,128)}, f32[1,1,8,8192]{3,2,1,0:T(8,128)}) custom-call(s32[24]{0:T(128)S(1)} %bitcast.9, f32[16,1,128]{2,1,0:T(1,128)S(1)} %all_to_all.33.squares, bf16[32,72,128]{2,1,0:T(8,128)(2,1)S(1)} %all_to_all.32.received, ...), custom_call_target="tpu_custom_call" | custom-call | tf_op jit(solution)/shard_map/finish/pallas_call | solution.py:344
  (1 shorter events, 0.0 us)
Async XLA Ops:
  19.1 17.1 %copy-start = (f32[1,1,8,8192]{3,2,1,0:T(8,128)S(1)}, f32[1,1,8,8192]{3,2,1,0:T(8,128)}, u32[]{:S(2)}) copy-start(f32[1,1,8,8192]{3,2,1,0:T(8,128)} %master.1) | copy-start | bytes 786436
  19.1 17.1 %copy-start.1 = (f32[1,1,8,8192]{3,2,1,0:T(8,128)S(1)}, f32[1,1,8,8192]{3,2,1,0:T(8,128)}, u32[]{:S(2)}) copy-start(f32[1,1,8,8192]{3,2,1,0:T(8,128)} %moment.1) | copy-start | bytes 786436
  19.1 17.1 %copy-start.2 = (f32[1,1,8,8192]{3,2,1,0:T(8,128)S(1)}, f32[1,1,8,8192]{3,2,1,0:T(8,128)}, u32[]{:S(2)}) copy-start(f32[1,1,8,8192]{3,2,1,0:T(8,128)} %second.1) | copy-start | bytes 786436
  19.1 17.1 %copy-start.4 = (s32[1,24]{1,0:T(1,128)S(1)}, s32[1,24]{1,0:T(1,128)}, u32[]{:S(2)}) copy-start(s32[1,24]{1,0:T(1,128)} %param.7) | copy-start | bytes 292
  91.6 17.8 %copy-start.3 = (f32[1,1,8,8192]{3,2,1,0:T(8,128)S(1)}, f32[1,1,8,8192]{3,2,1,0:T(8,128)}, u32[]{:S(2)}) copy-start(f32[1,1,8,8192]{3,2,1,0:T(8,128)} %average.1) | copy-start | bytes 786436
